TPU v7x, 128 devices: a whole 4x4x4 slice. The times are simulated.
128 devices in a mesh: tm: 8 (over x, z_lo), height: 8 (over z_hi, y), heads: 2 (over core).
Axes of the slice: x: 4, y: 4, z: 4 (z_hi: 2, z_lo: 2; z = z_hi * 2 + z_lo), core: 2. Of those that a mesh axis runs over, the one named last changes fastest.
Arguments:
- query_latent: bfloat16 [8, 8, 4, 128, 1536], P('tm', 'height', None, None, 'heads'), may hold values from -19 to 19
- key_latent: bfloat16 [8, 8, 4, 128, 1536], P('tm', 'height', None, None, 'heads'), may hold values from -19 to 19
- value_latent: bfloat16 [8, 8, 4, 128, 1536], P('tm', 'height', None, None, 'heads'), may hold values from -6 to 6
- grad_latent: bfloat16 [8, 8, 4, 128, 1536], P('tm', 'height', None, None, 'heads'), may hold values from -6 to 6
- tile_lists: int32 [8, 8, 4, 27], P('tm', 'height'), may hold values from -1 to 255, as said below
- text_query: bfloat16 [256, 1536], P(None, 'heads'), may hold values from -19 to 19
- text_key: bfloat16 [256, 1536], P(None, 'heads'), may hold values from -6 to 6
- text_value: bfloat16 [256, 1536], P(None, 'heads'), may hold values from -6 to 6
- grad_text: bfloat16 [256, 1536], P(None, 'heads'), may hold values from -6 to 6
- text_mask: int32 [256], replicated, may hold values 0 or 1
Outputs:
- out_latent: bfloat16 [8, 8, 4, 128, 1536], P('tm', 'height', None, None, 'heads')
- grad_q_latent: bfloat16 [8, 8, 4, 128, 1536], P('tm', 'height', None, None, 'heads')
- grad_k_latent: bfloat16 [8, 8, 4, 128, 1536], P('tm', 'height', None, None, 'heads')
- grad_v_latent: bfloat16 [8, 8, 4, 128, 1536], P('tm', 'height', None, None, 'heads')
- out_text: bfloat16 [256, 1536], P(None, 'heads')
- grad_q_text: bfloat16 [256, 1536], P(None, 'heads')
- grad_k_text: bfloat16 [256, 1536], P(None, 'heads')
- grad_v_text: bfloat16 [256, 1536], P(None, 'heads')
Inputs may be any that keep to these rules, and one draw needn't show every extreme that they name: `tile_lists`: entry 9 * a + 3 * b + c of query tile (f, r, w), a, b, c in 0..2, is -1 if frame tile f + a - 1 or row tile r + b - 1 lies outside the grid, else the index of tile (f + a - 1, r + b - 1, s + c), where s is an integer with max(0, w - 2) <= s <= min(w, 1) chosen per query tile and pair (a, b).
All inputs are finite; a program needn't handle non-finite values.
Results may differ from a plain program's by a relative error of at most 0.04.
Values may be sent and summed in bfloat16 or wider, within the bound.
A program may use at most 192 MiB of HBM per device.

v0:
```python
import math

import jax
import jax.numpy as jnp
from jax import lax
from jax.sharding import PartitionSpec as P

HD = 128


def extended(block, sides, width):
    for axis, dim in sides:
        count = lax.axis_size(axis)
        forward = [(i, i + 1) for i in range(count - 1)]
        backward = [(target, source) for source, target in forward]
        low = lax.ppermute(
            lax.slice_in_dim(block, block.shape[dim] - width, None, axis=dim), axis, forward
        )
        high = lax.ppermute(lax.slice_in_dim(block, 0, width, axis=dim), axis, backward)
        block = jnp.concatenate([low, block, high], axis=dim)
    return block


def from_behind(block, axis, distance):
    devices = range(lax.axis_size(axis))
    route = [(i - distance, i) for i in devices if i - distance in devices]
    return lax.ppermute(block, axis, route)


def window_pass(
    query,
    padded,
    tile_lists,
    key_text,
    value_text,
    text_on,
    grad_out,
    start_t,
    start_h,
    rows_tiles,
    head_dim,
    score_scale,
):
    frames, rows, width_tiles, tile, channels = query.shape
    heads = channels // head_dim
    groups = frames * rows
    block_rows = width_tiles * tile
    span = 9 * width_tiles * tile
    lists = tile_lists.reshape(frames, rows, width_tiles, 3, 3, 3)
    offsets = jnp.arange(3, dtype=jnp.int32) - 1
    frame_near = start_t + jnp.arange(frames, dtype=jnp.int32)[:, None] + offsets[None, :]
    row_near = start_h + jnp.arange(rows, dtype=jnp.int32)[:, None] + offsets[None, :]
    columns = jnp.arange(width_tiles, dtype=jnp.int32)
    expected = (
        frame_near[:, None, :, None, None] * rows_tiles + row_near[None, :, None, :, None]
    ) * width_tiles + columns[None, None, None, None, :]
    matches = (lists[..., None] == expected[:, :, None, :, :, None, :]) & (lists[..., None] >= 0)
    key_on = jnp.any(matches, axis=5).reshape(groups, width_tiles, 9 * width_tiles)
    key_on = jnp.repeat(key_on, tile, axis=2)
    query_groups = query.reshape(groups, block_rows, channels)
    grad_groups = grad_out.reshape(groups, block_rows, channels)

    def one_group(carry, inputs):
        totals, text_dk, text_dv = carry
        index, query_block, grad_block, mask_block = inputs
        nearby = padded.reshape(2, span, channels)
        on_rows = mask_block[:, None, :]

        def one_head(state, head):
            result_all, grad_q_all, grad_kv, words_dk, words_dv = state
            offset = head * head_dim

            def cut(array):
                return lax.dynamic_slice_in_dim(array, offset, head_dim, array.ndim - 1)

            query_head = cut(query_block)
            grad_head = cut(grad_block)
            key_head = cut(nearby[0])
            value_head = cut(nearby[1])
            key_words = cut(key_text)
            value_words = cut(value_text)
            score_window = (
                jnp.einsum("id,jd->ij", query_head, key_head, preferred_element_type=jnp.float32)
                * score_scale
            )
            score_window = jnp.where(
                on_rows, score_window.reshape(width_tiles, tile, span), -jnp.inf
            ).reshape(block_rows, span)
            score_words = (
                jnp.einsum("id,jd->ij", query_head, key_words, preferred_element_type=jnp.float32)
                * score_scale
            )
            score_words = jnp.where(text_on[None, :], score_words, -jnp.inf)
            peak = jnp.maximum(jnp.max(score_window, -1), jnp.max(score_words, -1))
            total = jnp.sum(jnp.exp(score_window - peak[:, None]), -1) + jnp.sum(
                jnp.exp(score_words - peak[:, None]), -1
            )
            log_total = (peak + jnp.log(total))[:, None]
            prob_window = jnp.exp(score_window - log_total)
            prob_words = jnp.exp(score_words - log_total)
            weight_window = prob_window.astype(jnp.bfloat16)
            weight_words = prob_words.astype(jnp.bfloat16)
            result = jnp.dot(weight_window, value_head, preferred_element_type=jnp.float32)
            result = (
                result + jnp.dot(weight_words, value_words, preferred_element_type=jnp.float32)
            ).astype(jnp.bfloat16)
            row_delta = jnp.sum(grad_head.astype(jnp.float32) * result.astype(jnp.float32), -1)[
                :, None
            ]
            dot_window = jnp.einsum(
                "id,jd->ij", grad_head, value_head, preferred_element_type=jnp.float32
            )
            dot_words = jnp.einsum(
                "id,jd->ij", grad_head, value_words, preferred_element_type=jnp.float32
            )
            dscore_window = (prob_window * (dot_window - row_delta)).astype(jnp.bfloat16)
            dscore_words = (prob_words * (dot_words - row_delta)).astype(jnp.bfloat16)
            grad_query = jnp.dot(dscore_window, key_head, preferred_element_type=jnp.float32)
            grad_query = (
                grad_query + jnp.dot(dscore_words, key_words, preferred_element_type=jnp.float32)
            ) * score_scale
            grad_keys = (
                jnp.einsum(
                    "ij,id->jd", dscore_window, query_head, preferred_element_type=jnp.float32
                )
                * score_scale
            )
            grad_values = jnp.einsum(
                "ij,id->jd", weight_window, grad_head, preferred_element_type=jnp.float32
            )
            added_dk = (
                jnp.einsum(
                    "ij,id->jd", dscore_words, query_head, preferred_element_type=jnp.float32
                )
                * score_scale
            )
            added_dv = jnp.einsum(
                "ij,id->jd", weight_words, grad_head, preferred_element_type=jnp.float32
            )
            result_all = lax.dynamic_update_slice_in_dim(result_all, result, offset, 1)
            grad_q_all = lax.dynamic_update_slice_in_dim(
                grad_q_all, grad_query.astype(jnp.bfloat16), offset, 1
            )
            grad_kv = lax.dynamic_update_slice_in_dim(
                grad_kv, jnp.stack([grad_keys, grad_values]), offset, 2
            )
            words_dk = lax.dynamic_update_slice_in_dim(
                words_dk, cut(words_dk) + added_dk, offset, 1
            )
            words_dv = lax.dynamic_update_slice_in_dim(
                words_dv, cut(words_dv) + added_dv, offset, 1
            )
            return ((result_all, grad_q_all, grad_kv, words_dk, words_dv), None)

        start_state = (
            jnp.zeros((block_rows, channels), jnp.bfloat16),
            jnp.zeros((block_rows, channels), jnp.bfloat16),
            jnp.zeros((2, span, channels), jnp.float32),
            text_dk,
            text_dv,
        )
        state, _ = lax.scan(one_head, start_state, jnp.arange(heads, dtype=jnp.int32))
        result_all, grad_q_all, grad_kv, text_dk, text_dv = state
        share = grad_kv.reshape(2, 3, 3, width_tiles, tile, channels)
        current = totals
        totals = current + share
        return ((totals, text_dk, text_dv), (result_all, grad_q_all))

    zero_pad = jnp.zeros((2, frames + 2, rows + 2, width_tiles, tile, channels), jnp.float32)
    zero_text = jnp.zeros((key_text.shape[0], channels), jnp.float32)
    carry, stacked = lax.scan(
        one_group,
        (zero_pad, zero_text, zero_text),
        (jnp.arange(groups, dtype=jnp.int32), query_groups, grad_groups, key_on),
    )
    totals, text_dk, text_dv = carry
    return (
        totals,
        text_dk,
        text_dv,
        stacked[0].reshape(query.shape),
        stacked[1].reshape(query.shape),
    )


def body(
    query_latent,
    key_latent,
    value_latent,
    grad_latent,
    tile_lists,
    text_query,
    text_key,
    text_value,
    grad_text,
    text_mask,
):
    frames, rows, width_tiles, tile, channels = query_latent.shape
    head_dim = HD
    heads = channels // head_dim
    score_scale = 1.0 / math.sqrt(head_dim)
    text_on = text_mask > 0
    key_text = text_key.reshape(-1, heads, head_dim)
    value_text = text_value.reshape(-1, heads, head_dim)
    query_text = text_query.reshape(-1, heads, head_dim)
    grad_words = grad_text.reshape(-1, heads, head_dim)
    both = jnp.stack([key_latent, value_latent])
    padded = extended(both, (("tm", 1), ("height", 2)), 1)
    start_t = lax.axis_index("tm") * frames
    start_h = lax.axis_index("height") * rows
    rows_tiles = rows * lax.axis_size("height")
    share, text_dk, text_dv, out_latent, grad_q_latent = window_pass(
        query_latent,
        padded,
        tile_lists,
        text_key,
        text_value,
        text_on,
        grad_latent,
        start_t,
        start_h,
        rows_tiles,
        head_dim,
        score_scale,
    )
    own_keys = key_latent.reshape(-1, heads, head_dim)
    own_values = value_latent.reshape(-1, heads, head_dim)
    score_own = (
        jnp.einsum("ihd,jhd->hij", query_text, own_keys, preferred_element_type=jnp.float32)
        * score_scale
    )
    score_words = (
        jnp.einsum("ihd,jhd->hij", query_text, key_text, preferred_element_type=jnp.float32)
        * score_scale
    )
    score_words = jnp.where(text_on[None, None, :], score_words, -jnp.inf)
    local_peak = jnp.max(score_own, -1)
    peak = lax.pmax(local_peak, ("tm", "height"))
    peak = jnp.maximum(peak, jnp.max(score_words, -1))
    local_total = jnp.sum(jnp.exp(score_own - peak[..., None]), -1)
    total = lax.psum(local_total, ("tm", "height"))
    total = total + jnp.sum(jnp.exp(score_words - peak[..., None]), -1)
    log_total = (peak + jnp.log(total))[..., None]
    prob_own = jnp.exp(score_own - log_total)
    prob_words = jnp.exp(score_words - log_total)
    weight_own = prob_own.astype(jnp.bfloat16)
    weight_words = prob_words.astype(jnp.bfloat16)
    numer = jnp.einsum(
        "hij,jhd->ihd", weight_own, own_values, preferred_element_type=jnp.float32
    ).reshape(-1, channels)
    numer = lax.psum(numer, ("tm", "height"))
    words_part = jnp.einsum(
        "hij,jhd->ihd", weight_words, value_text, preferred_element_type=jnp.float32
    ).reshape(-1, channels)
    out_text = (numer + words_part).astype(jnp.bfloat16)
    row_delta = jnp.transpose(
        jnp.sum(
            grad_words.astype(jnp.float32)
            * out_text.reshape(-1, heads, head_dim).astype(jnp.float32),
            -1,
        ),
        (1, 0),
    )[..., None]
    dscore_own = (
        prob_own
        * (
            jnp.einsum("ihd,jhd->hij", grad_words, own_values, preferred_element_type=jnp.float32)
            - row_delta
        )
    ).astype(jnp.bfloat16)
    dscore_words = (
        prob_words
        * (
            jnp.einsum("ihd,jhd->hij", grad_words, value_text, preferred_element_type=jnp.float32)
            - row_delta
        )
    ).astype(jnp.bfloat16)
    query_part = (
        jnp.einsum("hij,jhd->ihd", dscore_own, own_keys, preferred_element_type=jnp.float32)
        * score_scale
    )
    own_dk = (
        jnp.einsum("hij,ihd->jhd", dscore_own, query_text, preferred_element_type=jnp.float32)
        * score_scale
    )
    own_dv = jnp.einsum("hij,ihd->jhd", weight_own, grad_words, preferred_element_type=jnp.float32)
    summed_q, summed_k, summed_v = lax.psum(
        (query_part.reshape(-1, channels), text_dk, text_dv), ("tm", "height")
    )
    words_q = (
        jnp.einsum("hij,jhd->ihd", dscore_words, key_text, preferred_element_type=jnp.float32)
        * score_scale
    )
    words_k = (
        jnp.einsum("hij,ihd->jhd", dscore_words, query_text, preferred_element_type=jnp.float32)
        * score_scale
    )
    words_v = jnp.einsum(
        "hij,ihd->jhd", weight_words, grad_words, preferred_element_type=jnp.float32
    )
    grad_q_text = (summed_q + words_q.reshape(-1, channels)).astype(jnp.bfloat16)
    grad_k_text = (summed_k + words_k.reshape(-1, channels)).astype(jnp.bfloat16)
    grad_v_text = (summed_v + words_v.reshape(-1, channels)).astype(jnp.bfloat16)
    rims = share.astype(jnp.bfloat16)
    from_next = from_behind(rims[:, 0], "tm", -1)
    from_prev = from_behind(rims[:, frames + 1], "tm", 1)
    middle = rims[:, 1 : frames + 1].astype(jnp.float32)
    middle = middle.at[:, frames - 1].add(from_next.astype(jnp.float32))
    middle = middle.at[:, 0].add(from_prev.astype(jnp.float32))
    low_edge = from_behind(middle[:, :, 0].astype(jnp.bfloat16), "height", -1).astype(jnp.float32)
    high_edge = from_behind(middle[:, :, rows + 1].astype(jnp.bfloat16), "height", 1).astype(
        jnp.float32
    )
    inner = middle[:, :, 1 : rows + 1]
    inner = inner.at[:, :, rows - 1].add(low_edge)
    inner = inner.at[:, :, 0].add(high_edge)
    grad_k_latent = (inner[0] + own_dk.reshape(query_latent.shape)).astype(jnp.bfloat16)
    grad_v_latent = (inner[1] + own_dv.reshape(query_latent.shape)).astype(jnp.bfloat16)
    return (
        out_latent,
        grad_q_latent,
        grad_k_latent,
        grad_v_latent,
        out_text,
        grad_q_text,
        grad_k_text,
        grad_v_text,
    )


def solution(mesh):
    in_specs = (
        P("tm", "height", None, None, "heads"),
        P("tm", "height", None, None, "heads"),
        P("tm", "height", None, None, "heads"),
        P("tm", "height", None, None, "heads"),
        P("tm", "height", None, None),
        P(None, "heads"),
        P(None, "heads"),
        P(None, "heads"),
        P(None, "heads"),
        P(),
    )
    out_specs = (
        P("tm", "height", None, None, "heads"),
        P("tm", "height", None, None, "heads"),
        P("tm", "height", None, None, "heads"),
        P("tm", "height", None, None, "heads"),
        P(None, "heads"),
        P(None, "heads"),
        P(None, "heads"),
        P(None, "heads"),
    )
    return jax.shard_map(body, mesh=mesh, in_specs=in_specs, out_specs=out_specs, check_vma=False)
```

profile of v0, /device:TPU:0, one launch (start us, length us, event | category | flops | bytes accessed | tf_op | source)
XLA Modules:
  0.0 1179.2 jit_solution(6203950739992806068)
XLA Ops:
  14.8 32.3 %collective-permute-done.1 = bf16[2,1,1,4,128,768]{5,4,3,2,1,0:T(8,128)(2,1)S(1)} collective-permute-done((bf16[2,1,1,4,128,768]{5,4,3,2,1,0:T(8,128)(2,1)S(1)}, bf16[2,1,1,4,128,768]{5,4,3,2,1,0:T(8,128)(2,1)S(1)}, u32[]{:S(2)}, u32[]{:S(2)}) %collective-permute-start.1) | collective-permute-done | bytes 1572896 | tf_op jit(solution)/shard_map/ppermute | solution.py:19
  47.2 33.9 %collective-permute-done = bf16[2,1,1,4,128,768]{5,4,3,2,1,0:T(8,128)(2,1)S(1)} collective-permute-done((bf16[2,1,1,4,128,768]{5,4,3,2,1,0:T(8,128)(2,1)S(1)}, bf16[2,1,1,4,128,768]{5,4,3,2,1,0:T(8,128)(2,1)S(1)}, u32[]{:S(2)}, u32[]{:S(2)}) %collective-permute-start) | collective-permute-done | bytes 1572896 | tf_op jit(solution)/shard_map/ppermute | solution.py:16
  85.0 6.8 collective-permute-start.2
  92.6 97.1 %collective-permute-done.3 = bf16[2,3,1,4,128,768]{5,4,3,2,1,0:T(8,128)(2,1)} collective-permute-done((bf16[2,3,1,4,128,768]{5,4,3,2,1,0:T(8,128)(2,1)}, bf16[2,3,1,4,128,768]{5,4,3,2,1,0:T(8,128)(2,1)}, u32[]{:S(2)}, u32[]{:S(2)}) %collective-permute-start.3) | collective-permute-done | bytes 4718624 | tf_op jit(solution)/shard_map/ppermute | solution.py:19
  190.8 9.9 pad_maximum_fusion
  202.6 6.0 broadcast.261
  208.7 222.0 %while.38 = (s32[]{:T(128)}, bf16[512,768]{1,0:T(8,128)(2,1)}, bf16[512,768]{1,0:T(8,128)(2,1)}, bf16[2,4608,768]{2,1,0:T(8,128)(2,1)}, f32[256,768]{1,0:T(8,128...) while((s32[]{:T(128)}, bf16[512,768]{1,0:T(8,128)(2,1)}, ...), condition=%wide.region_7.8_spmd.clone, body=%wide.region_1.7_spmd.clone.sunk | while | flops 3864165376 | bytes 231990336 | solution.py:162
  212.3 5.8 fusion.163
  231.0 5.7 multiply_convert_fusion.4
  249.1 5.8 fusion.163
  267.9 5.7 multiply_convert_fusion.4
  286.0 5.8 fusion.163
  304.8 5.7 multiply_convert_fusion.4
  323.0 5.8 fusion.163
  341.7 5.7 multiply_convert_fusion.4
  359.9 5.8 fusion.163
  397.0 5.8 fusion.163
  430.8 9.1 slice_bitcast_fusion.1
  439.9 6.8 collective-permute-start.5
  455.4 229.5 %pmax.7 = f32[6,256]{1,0:T(8,128)} all-reduce(f32[6,256]{1,0:T(8,128)S(1)} %get-tuple-element.312), channel_id=1, replica_groups=mesh['tm'=8,'height'=8,'heads'=2] {'tm','height'}, use_global_device_ids=true, to_apply=%region_9.10 | all-reduce | flops 1536 | bytes 12288 | tf_op jit(solution)/shard_map/pmax | solution.py:238
  689.2 176.6 %psum.35 = f32[6,256]{1,0:T(8,128)} all-reduce(f32[6,256]{1,0:T(8,128)S(1)} %exponential_reduce_fusion.2), channel_id=1, replica_groups=mesh['tm'=8,'height'=8,'heads'=2] {'tm','height'}, use_global_device_ids=true, to_apply=%region_12.13 | all-reduce | flops 1536 | bytes 12288 | tf_op jit(solution)/shard_map/psum | solution.py:241
  887.2 106.0 %all-reduce.4.cloned.1.call-done = f32[256,768]{0,1:T(8,128)} async-done(((f32[256,768]{0,1:T(8,128)}), f32[256,768]{0,1:T(8,128)}) %all-reduce.4.cloned.1.call-update) | async-done | bytes 786448 | tf_op jit(solution)/shard_map/psum | solution.py:251
  1009.0 13.5 %fusion.83 = (bf16[2,1,3,4,128,768]{5,4,3,2,0,1:T(8,128)(2,1)}, f32[2,1,3,4,128,768]{5,4,3,2,0,1:T(8,128)}) fusion(bf16[2,3,4,128,768]{4,3,2,1,0:T(8,128)(2,1)} %collective-permute-done.5, bf16[2,3,4,128,768]{4,3,2,1,0:T(8,128)(2,1)} %collective-permute-done.4, bf16[2,3,3,4,128,768]{5,4,3,2,1,0:T(8,128)(2,1)} %bitcast.197), kind=kLoop, calls=%fused_computation.120 | loop fusion | flops 14155776 | bytes 28311552 | tf_op jit(solution)/shard_map/convert.6
  1038.3 124.1 %all-reduce.6.cloned.1.call-done = (f32[256,768]{1,0:T(8,128)}, f32[256,768]{1,0:T(8,128)}, f32[256,768]{1,0:T(8,128)}) async-done(((f32[256,768]{1,0:T(8,128)}, f32[256,768]{1,0:T(8,128)}, f32[256,768]{1,0:T(8,128)}), (f32[256,768]{1,0:T(8,128)}, f32[256,768]{1,0:T(8,128)}, f32[256,768]{1,0:T(8,128)})) %all-reduce.6.cloned.1.call-update) | async-done | bytes 2359312 | tf_op jit(solution)/shard_map/psum | solution.py:287
  (338 shorter events, 250.2 us)
Async XLA Ops:
  7.2 73.9 %copy-start.8 = (bf16[1,1,4,128,768]{4,3,2,1,0:T(8,128)(2,1)S(1)}, bf16[1,1,4,128,768]{4,3,2,1,0:T(8,128)(2,1)}, u32[]{:S(2)}) copy-start(bf16[1,1,4,128,768]{4,3,2,1,0:T(8,128)(2,1)} %param.22) | copy-start | bytes 2359300
  7.2 73.9 %copy-start.6 = (bf16[1,1,4,128,768]{4,3,2,1,0:T(8,128)(2,1)S(1)}, bf16[1,1,4,128,768]{4,3,2,1,0:T(8,128)(2,1)}, u32[]{:S(2)}) copy-start(bf16[1,1,4,128,768]{4,3,2,1,0:T(8,128)(2,1)} %param.21) | copy-start | bytes 2359300
  7.2 986.0 %all-reduce.4.cloned.1.call-start = ((), (), s32[]{:S(2)}) async-start(), calls=%async_computation | async-start | bytes 1572864 | tf_op jit(solution)/shard_map/psum | solution.py:251
  8.9 82.9 %copy-start.24 = (s32[1,1,4,27]{3,2,1,0:T(4,128)S(1)}, s32[1,1,4,27]{3,2,1,0:T(4,128)}, u32[]{:S(2)}) copy-start(s32[1,1,4,27]{3,2,1,0:T(4,128)} %param.24) | copy-start | bytes 1300
  8.9 83.7 %copy-start.25 = (s32[256]{0:T(256)S(1)}, s32[256]{0:T(256)}, u32[]{:S(2)}) copy-start(s32[256]{0:T(256)} %param.29) | copy-start | bytes 3076
  8.9 38.3 %collective-permute-start.1 = (bf16[2,1,1,4,128,768]{5,4,3,2,1,0:T(8,128)(2,1)S(1)}, bf16[2,1,1,4,128,768]{5,4,3,2,1,0:T(8,128)(2,1)S(1)}, u32[]{:S(2)}, u32[]{:S(2)}) collective-permute-start(bf16[2,1,1,4,128,768]{5,4,3,2,1,0:T(8,128)(2,1)S(1)} %pad_maximum_fusion.2), channel_id=1, source_target_pairs={{16,0},{32,16},{48,32},{64,48},{80,64},{96,80},{112,96},{17,1},{33... | collective-permute-start | bytes 4718600 | tf_op jit(solution)/shard_map/ppermute | solution.py:19
  10.2 70.9 %collective-permute-start = (bf16[2,1,1,4,128,768]{5,4,3,2,1,0:T(8,128)(2,1)S(1)}, bf16[2,1,1,4,128,768]{5,4,3,2,1,0:T(8,128)(2,1)S(1)}, u32[]{:S(2)}, u32[]{:S(2)}) collective-permute-start(bf16[2,1,1,4,128,768]{5,4,3,2,1,0:T(8,128)(2,1)S(1)} %pad_maximum_fusion.2), channel_id=1, source_target_pairs={{0,16},{16,32},{32,48},{48,64},{64,80},{80,96},{96,112},{1,17},{17... | collective-permute-start | bytes 4718600 | tf_op jit(solution)/shard_map/ppermute | solution.py:16
  83.7 105.9 %collective-permute-start.3 = (bf16[2,3,1,4,128,768]{5,4,3,2,1,0:T(8,128)(2,1)}, bf16[2,3,1,4,128,768]{5,4,3,2,1,0:T(8,128)(2,1)}, u32[]{:S(2)}, u32[]{:S(2)}) collective-permute-start(bf16[2,3,1,4,128,768]{5,4,3,2,1,0:T(8,128)(2,1)} %pad_maximum_fusion.1), channel_id=1, source_target_pairs={{2,0},{4,2},{6,4},{8,6},{10,8},{12,10},{14,12},{3,1},{5,3},{7,5},{... | collective-permute-start | bytes 14155784 | tf_op jit(solution)/shard_map/ppermute | solution.py:19
  85.0 105.8 %collective-permute-start.2 = (bf16[2,3,1,4,128,768]{5,4,3,2,1,0:T(8,128)(2,1)}, bf16[2,3,1,4,128,768]{5,4,3,2,1,0:T(8,128)(2,1)}, u32[]{:S(2)}, u32[]{:S(2)}) collective-permute-start(bf16[2,3,1,4,128,768]{5,4,3,2,1,0:T(8,128)(2,1)} %pad_maximum_fusion.1), channel_id=1, source_target_pairs={{0,2},{2,4},{4,6},{6,8},{8,10},{10,12},{12,14},{1,3},{3,5},{5,7},{... | collective-permute-start | bytes 14155784 | tf_op jit(solution)/shard_map/ppermute | solution.py:16
  229.8 10.4 slice-start
  266.6 10.4 slice-start
  303.5 10.4 slice-start
  340.4 10.4 slice-start
  414.5 10.4 slice-start
  430.8 17.1 %copy-start.7 = (bf16[1,1,4,128,768]{4,3,2,1,0:T(8,128)(2,1)S(1)}, bf16[1,1,4,128,768]{4,3,2,1,0:T(8,128)(2,1)}, u32[]{:S(2)}) copy-start(bf16[1,1,4,128,768]{4,3,2,1,0:T(8,128)(2,1)} %param.21) | copy-start | bytes 2359300
  430.8 19.7 %copy-start.9 = (bf16[1,1,4,128,768]{4,3,2,1,0:T(8,128)(2,1)S(1)}, bf16[1,1,4,128,768]{4,3,2,1,0:T(8,128)(2,1)}, u32[]{:S(2)}) copy-start(bf16[1,1,4,128,768]{4,3,2,1,0:T(8,128)(2,1)} %param.22) | copy-start | bytes 2359300
  439.9 11.2 copy-start.23
  439.9 569.1 %collective-permute-start.5 = (bf16[2,3,4,128,768]{4,3,2,1,0:T(8,128)(2,1)}, bf16[2,3,4,128,768]{4,3,2,1,0:T(8,128)(2,1)}, u32[]{:S(2)}, u32[]{:S(2)}) collective-permute-start(bf16[2,3,4,128,768]{4,3,2,1,0:T(8,128)(2,1)} %get-tuple-element.307), channel_id=1, source_target_pairs={{0,16},{16,32},{32,48},{48,64},{64,80},{80,96},{96,112},{1,17},{17... | collective-permute-start | bytes 14155784 | tf_op jit(solution)/shard_map/ppermute | solution.py:27
  446.6 562.4 %collective-permute-start.4 = (bf16[2,3,4,128,768]{4,3,2,1,0:T(8,128)(2,1)}, bf16[2,3,4,128,768]{4,3,2,1,0:T(8,128)(2,1)}, u32[]{:S(2)}, u32[]{:S(2)}) collective-permute-start(bf16[2,3,4,128,768]{4,3,2,1,0:T(8,128)(2,1)} %get-tuple-element.306), channel_id=1, source_target_pairs={{16,0},{32,16},{48,32},{64,48},{80,64},{96,80},{112,96},{17,1},{33... | collective-permute-start | bytes 14155784 | tf_op jit(solution)/shard_map/ppermute | solution.py:27
  451.2 233.7 %copy-start.10 = (bf16[256,768]{0,1:T(8,128)(2,1)}, bf16[256,768]{0,1:T(8,128)(2,1)S(1)}, u32[]{:S(2)}) copy-start(bf16[256,768]{0,1:T(8,128)(2,1)S(1)} %copy.103) | copy-start | bytes 1179652
  871.1 291.4 %all-reduce.6.cloned.1.call-start = ((), (), s32[]{:S(2)}) async-start(), calls=%async_computation.1 | async-start | bytes 4718592 | tf_op jit(solution)/shard_map/psum | solution.py:287
  1026.5 140.9 %collective-permute-start.7 = (bf16[2,1,4,128,768]{4,3,2,0,1:T(8,128)(2,1)}, bf16[2,1,4,128,768]{4,3,2,0,1:T(8,128)(2,1)}, u32[]{:S(2)}, u32[]{:S(2)}) collective-permute-start(bf16[2,1,4,128,768]{4,3,2,0,1:T(8,128)(2,1)} %get-tuple-element.309), channel_id=1, source_target_pairs={{0,2},{2,4},{4,6},{6,8},{8,10},{10,12},{12,14},{1,3},{3,5},{5,7},{... | collective-permute-start | bytes 4718600 | tf_op jit(solution)/shard_map/ppermute | solution.py:27
  1030.3 137.2 %collective-permute-start.6 = (bf16[2,1,4,128,768]{4,3,2,0,1:T(8,128)(2,1)}, bf16[2,1,4,128,768]{4,3,2,0,1:T(8,128)(2,1)}, u32[]{:S(2)}, u32[]{:S(2)}) collective-permute-start(bf16[2,1,4,128,768]{4,3,2,0,1:T(8,128)(2,1)} %get-tuple-element.308), channel_id=1, source_target_pairs={{2,0},{4,2},{6,4},{8,6},{10,8},{12,10},{14,12},{3,1},{5,3},{7,5},{... | collective-permute-start | bytes 4718600 | tf_op jit(solution)/shard_map/ppermute | solution.py:27
  1035.9 130.7 %copy-start.20 = (f32[256,768]{1,0:T(8,128)S(1)}, f32[256,768]{1,0:T(8,128)}, u32[]{:S(2)}) copy-start(f32[256,768]{1,0:T(8,128)} %copy.133) | copy-start | bytes 2359300
  (45 other events, 276.4 us)
Sparse Core Ops, SparseCore 0:
  871.2 121.9 all-reduce.3
  1003.9 158.4 all-reduce.5
where the time goes:
time: 1180 us
  blocking collectives  406 us (34%)
  waiting for transfers between devices  395 us (33%)
  matrix products  147 us (12%)
  local copies, waits for them, and re-layouts  120 us (10%)
  other arithmetic  64.7 us (5%)
  starting transfers between devices  27.1 us (2%)
  between operations  14.4 us (1%)
    pmax x1, blocking collectives, body(): peak = lax.pmax(local_peak, ('tm', 'height'))  230 us
    psum x1, blocking collectives, body(): total = lax.psum(local_total, ('tm', 'height'))  177 us
    ppermute x2, waiting for transfers between devices, extended(): lax.ppermute(lax.slice_in_dim(block, 0, width, axis=dim), axis, backward)  129 us
    psum x1, waiting for transfers between devices, body(): lax.psum((query_part.reshape(-1, channels), text_dk, text_dv), ('tm', 'he...  124 us
    psum x1, waiting for transfers between devices, body(): numer = lax.psum(numer, ('tm', 'height'))  106 us
    ppermute x2, waiting for transfers between devices, extended(): lax.ppermute(lax.slice_in_dim(block, block.shape[dim] - width, None, axis...  35 us
    slice x6, local copies, waits for them, and re-layouts, one_head(): value_head = cut(nearby[1])  34.7 us
    dot_general x6, matrix products, one_head(): jnp.einsum('id,jd->ij', grad_head, value_head, preferred_element_type=jnp...  34.2 us
  transfers between devices with their start and end apart: 10, of which 6 were waited for; matrix products, arithmetic and copies ran while one was open for 7% of the time, Pallas kernels for 0%

commit v1 on v0

v1 whole, which is shorter than its diff:
```python
import functools
import math

import jax
import jax.numpy as jnp
from jax import lax
from jax.experimental import pallas as pl
from jax.experimental.pallas import tpu as pltpu
from jax.sharding import PartitionSpec as P

HD = 128
NEG = -1e30
F32 = jnp.float32
BF16 = jnp.bfloat16
MESH = pl.DeviceIdType.MESH


def mm_nt(a, b):
    return lax.dot_general(a, b, (((1,), (1,)), ((), ())), preferred_element_type=F32)


def mm_tn(a, b):
    return lax.dot_general(a, b, (((0,), (0,)), ((), ())), preferred_element_type=F32)


def mm_nn(a, b):
    return jnp.dot(a, b, preferred_element_type=F32)


def window_kernel(
    nx,
    ny,
    q_ref,
    k_ref,
    v_ref,
    g_ref,
    mask_ref,
    tk_ref,
    tv_ref,
    tm_ref,
    out_ref,
    dq_ref,
    dk_ref,
    dv_ref,
    td_ref,
    kv,
    qg,
    mask,
    p_mid,
    p_side,
    p_text,
    m_saved,
    m_run,
    l_run,
    d_row,
    o_t,
    dq_t,
    share,
    g1r,
    g2r,
    fin,
    sem_loc,
    sem_r1s,
    sem_r1r,
    sem_mask,
    sem_r2s,
    sem_r2r,
    sem_r3s,
    sem_r3r,
    sem_g1s,
    sem_g1r,
    sem_g2s,
    sem_g2r,
    sem_g3s,
    sem_g3r,
    sem_out,
):
    bq = q_ref.shape[0]
    tile = bq // 4
    heads = q_ref.shape[1] // HD
    nh = heads // 2
    both = 2 * bq
    scale = 1.0 / math.sqrt(HD)
    c2 = scale * math.log2(math.e)

    t = lax.axis_index("tm")
    h = lax.axis_index("height")
    c = lax.axis_index("heads")
    x = t // 2
    zl = t % 2
    zh = h // ny
    half = (zl + zh) % 2
    other = 1 - half
    rows_all = 2 * ny

    def at_height(hh):
        return (2 * x + (half + hh // ny) % 2, hh, c)

    partner = (2 * x + 1 - zl, h, c)
    left = (t - 2, h, c)
    right = (t + 2, h, c)
    up = at_height(h - 1)
    down = at_height(h + 1)
    has_left = x > 0
    has_right = x < nx - 1
    has_up = h > 0
    has_down = h < rows_all - 1

    barrier = pltpu.get_barrier_semaphore()
    greet = [
        (None, partner),
        (has_left, left),
        (has_right, right),
        (has_up, up),
        (has_down, down),
    ]
    for cond, dev in greet:
        def hello(dev=dev):
            pl.semaphore_signal(barrier, inc=1, device_id=dev, device_id_type=MESH)

        if cond is None:
            hello()
        else:
            pl.when(cond)(hello)
    count = (
        1
        + has_left.astype(jnp.int32)
        + has_right.astype(jnp.int32)
        + has_up.astype(jnp.int32)
        + has_down.astype(jnp.int32)
    )
    pl.semaphore_wait(barrier, count)

    def remote(src, dst, ssem, rsem, dev):
        return pltpu.make_async_remote_copy(
            src_ref=src, dst_ref=dst, send_sem=ssem, recv_sem=rsem,
            device_id=dev, device_id_type=MESH,
        )

    def head_cols(which, i):
        return pl.ds(pl.multiple_of((which * nh + i) * HD, HD), HD)

    ins = (q_ref, k_ref, v_ref, g_ref)
    outs = (out_ref, dq_ref, dk_ref, dv_ref)

    def landing(i, j):
        if j == 0:
            return qg.at[i, 0, pl.ds(pl.multiple_of(zl * bq, bq), bq)]
        if j == 3:
            return qg.at[i, 1, pl.ds(pl.multiple_of(zl * bq, bq), bq)]
        return kv.at[i, j - 1, 1, 1 + zl]

    def r1(i, j):
        return remote(
            ins[j].at[:, head_cols(other, i)], landing(i, j),
            sem_r1s.at[i, j], sem_r1r.at[i, j], partner,
        )

    def local_in(i, j):
        return pltpu.make_async_copy(
            ins[j].at[:, head_cols(half, i)], landing(i, j), sem_loc.at[i, j]
        )

    mask_cols = pl.ds(pl.multiple_of(zl * bq, bq), bq)
    mask_out = remote(mask_ref, mask.at[:, mask_cols], sem_mask.at[0], sem_mask.at[1], partner)
    mask_own = pltpu.make_async_copy(mask_ref, mask.at[:, mask_cols], sem_mask.at[2])

    def r2(i, d):
        return remote(
            kv.at[i, :, 1, pl.ds(1, 2)], kv.at[i, :, 2 - 2 * d, pl.ds(1, 2)],
            sem_r2s.at[i, d], sem_r2r.at[i, d], (up, down)[d],
        )

    def r3(i, r, d):
        return remote(
            kv.at[i, :, r, 1 + d], kv.at[i, :, r, 3 - 3 * d],
            sem_r3s.at[i, r, d], sem_r3r.at[i, r, d], (left, right)[d],
        )

    def g1(i, r, d):
        return remote(
            share.at[i, :, r, 3 * d], g1r.at[i, d, :, r],
            sem_g1s.at[i, r, d], sem_g1r.at[i, r, d], (left, right)[d],
        )

    def g2(i, d):
        return remote(
            share.at[i, :, 2 * d, pl.ds(1, 2)], g2r.at[i, d],
            sem_g2s.at[i, d], sem_g2r.at[i, d], (up, down)[d],
        )

    def g3(i, j):
        return remote(
            fin.at[i, j, pl.ds(pl.multiple_of((1 - zl) * bq, bq), bq)],
            outs[j].at[:, head_cols(half, i)],
            sem_g3s.at[i, j], sem_g3r.at[i, j], partner,
        )

    def local_out(i, j):
        return pltpu.make_async_copy(
            fin.at[i, j, pl.ds(pl.multiple_of(zl * bq, bq), bq)],
            outs[j].at[:, head_cols(half, i)], sem_out.at[i, j],
        )

    def row_on(r):
        return (h + r - 1 >= 0) & (h + r - 1 < rows_all)

    side_on = (has_left, has_right)
    vert_on = (has_up, has_down)

    def wait_r1(i):
        for j in range(4):
            local_in(i, j).wait()
            r1(i, j).wait_recv()

    def start_r2(i):
        for d in range(2):
            pl.when(vert_on[d])(lambda d=d: r2(i, d).start())

    def wait_r2(i):
        for d in range(2):
            pl.when(vert_on[1 - d])(lambda d=d: r2(i, d).wait_recv())

    def for_sides(i, rows, act, flip):
        for r in rows:
            for d in range(2):
                on = side_on[1 - d] if flip else side_on[d]
                if r != 1:
                    on = on & row_on(r)
                pl.when(on)(lambda r=r, d=d: act(i, r, d))

    def start_r3(i, rows):
        for_sides(i, rows, lambda i, r, d: r3(i, r, d).start(), False)

    def wait_r3(i):
        for_sides(i, (0, 1, 2), lambda i, r, d: r3(i, r, d).wait_recv(), True)

    @pl.loop(0, nh)
    def _(i):
        for j in range(4):
            r1(i, j).start()
            local_in(i, j).start()

    mask_out.start()
    mask_own.start()

    @pl.loop(0, nh)
    def _(i):
        @pl.when(jnp.logical_not(has_right))
        def _():
            g1r[i, 0] = jnp.zeros(g1r.shape[2:], BF16)

        @pl.when(jnp.logical_not(has_left))
        def _():
            g1r[i, 1] = jnp.zeros(g1r.shape[2:], BF16)

        @pl.when(jnp.logical_not(has_down))
        def _():
            g2r[i, 0] = jnp.zeros(g2r.shape[2:], BF16)

        @pl.when(jnp.logical_not(has_up))
        def _():
            g2r[i, 1] = jnp.zeros(g2r.shape[2:], BF16)

    mask_own.wait()
    mask_out.wait_recv()
    wait_r1(0)
    start_r2(0)
    start_r3(0, (1,))

    def online(s, v, save, qs, keep):
        m_old = m_run[0:1, qs]
        m_new = jnp.maximum(m_old, jnp.max(s, 0, keepdims=True))
        alpha = jnp.exp2(m_old - m_new)
        e = jnp.exp2(s - m_new)
        l_run[0:1, qs] = l_run[0:1, qs] * alpha + jnp.sum(e, 0, keepdims=True)
        m_run[0:1, qs] = m_new
        m_saved[pl.ds(save, 1), qs] = m_new
        w = e.astype(BF16)
        keep(w)
        o_t[:, qs] = o_t[:, qs] * alpha + mm_tn(v, w)

    def fwd(i, row, col, qs, keep):
        s = mm_nt(kv[i, 0, row, col], qg[i, 0, qs]) * c2
        at = (col * 3 + row) * 2
        first = mask[pl.ds(at, 1), qs]
        last = mask[pl.ds(at + 1, 1), qs]
        s = jnp.concatenate(
            [
                jnp.where(first > 0.5, s[:tile], NEG),
                s[tile : 3 * tile],
                jnp.where(last > 0.5, s[3 * tile :], NEG),
            ],
            axis=0,
        )
        online(s, kv[i, 1, row, col], col * 3 + row, qs, keep)

    def fwd_mid(i, row, col):
        def keep(w):
            p_mid[row, col - 1] = w

        fwd(i, row, col, pl.ds(0, both), keep)

    def fwd_side(i, row, d):
        def keep(w):
            p_side[row, d] = w

        fwd(i, row, 3 * d, pl.ds(d * bq, bq), keep)

    def back(w0, k, v, q, g, save, qs):
        f = jnp.exp2(m_saved[pl.ds(save, 1), qs] - m_run[0:1, qs]) * l_run[0:1, qs]
        dp = mm_nt(v, g)
        w = w0.astype(F32) * f
        ds = (w * (dp - d_row[0:1, qs])).astype(BF16)
        d_k = mm_nn(ds, q) * scale
        d_v = mm_nn(w.astype(BF16), g)
        dq_t[:, qs] += mm_tn(k, ds)
        return d_k, d_v

    def bwd(i, row, col, qs, w0):
        d_k, d_v = back(
            w0, kv[i, 0, row, col], kv[i, 1, row, col], qg[i, 0, qs], qg[i, 1, qs],
            col * 3 + row, qs,
        )
        share[i, 0, row, col] = d_k.astype(BF16)
        share[i, 1, row, col] = d_v.astype(BF16)

    def add_g1(i):
        for_sides(i, (0, 1, 2), lambda i, r, d: g1(i, r, d).wait_recv(), True)
        for r in (0, 2):
            @pl.when(row_on(r))
            def _(r=r):
                for a in range(2):
                    for d in range(2):
                        col = 2 - d
                        share[i, a, r, col] = (
                            share[i, a, r, col].astype(F32) + g1r[i, d, a, r].astype(F32)
                        ).astype(BF16)
        for d in range(2):
            pl.when(vert_on[d])(lambda d=d: g2(i, d).start())

    def add_g2(i):
        for d in range(2):
            pl.when(vert_on[1 - d])(lambda d=d: g2(i, d).wait_recv())
        for a in range(2):
            for s in range(2):
                total = (
                    share[i, a, 1, 1 + s].astype(F32)
                    + g1r[i, 1 - s, a, 1].astype(F32)
                    + g2r[i, 0, a, s].astype(F32)
                    + g2r[i, 1, a, s].astype(F32)
                )
                fin[i, 2 + a, s * bq : (s + 1) * bq] = total.astype(BF16)
        for j in (2, 3):
            g3(i, j).start()
            local_out(i, j).start()

    @pl.loop(0, nh)
    def _(i):
        m_run[0:1, :] = jnp.full((1, both), NEG, F32)
        l_run[0:1, :] = jnp.zeros((1, both), F32)
        o_t[...] = jnp.zeros(o_t.shape, F32)
        dq_t[...] = jnp.zeros(dq_t.shape, F32)

        @pl.loop(1, 3)
        def _(col):
            fwd_mid(i, 1, col)

        @pl.when(i == 0)
        def _():
            wait_r1(1)
            start_r2(1)
            start_r3(1, (1,))
            wait_r2(0)
            start_r3(0, (0, 2))

        @pl.loop(0, 4)
        def _(n):
            row = (n // 2) * 2

            @pl.when(row_on(row))
            def _():
                fwd_mid(i, row, 1 + n % 2)

        @pl.when(i == 0)
        def _():
            wait_r1(2)
            start_r2(2)
            start_r3(2, (1,))

        @pl.when(i < nh - 1)
        def _():
            wait_r2(i + 1)
            start_r3(i + 1, (0, 2))

        words = head_cols(half, i)
        s_text = jnp.where(
            tm_ref[:, 0:1] > 0.5, mm_nt(tk_ref[:, words], qg[i, 0]) * c2, NEG
        )

        def keep_text(w):
            p_text[...] = w

        online(s_text, tv_ref[:, words], 12, pl.ds(0, both), keep_text)

        @pl.when(i > 0)
        def _():
            add_g1(i - 1)

        wait_r3(i)
        for d in range(2):
            @pl.when(side_on[d])
            def _(d=d):
                @pl.loop(0, 3)
                def _(row):
                    @pl.when(row_on(row))
                    def _():
                        fwd_side(i, row, d)

        inv = 1.0 / l_run[0:1, :]
        l_run[0:1, :] = inv
        o_round = (o_t[...] * inv).astype(BF16).astype(F32)
        fin[i, 0] = o_round.T.astype(BF16)
        g_t = qg[i, 1].astype(F32).T
        d_row[0:1, :] = jnp.sum(o_round * g_t, 0, keepdims=True)
        g3(i, 0).start()
        local_out(i, 0).start()

        d_k, d_v = back(
            p_text[...], tk_ref[:, words], tv_ref[:, words], qg[i, 0], qg[i, 1],
            12, pl.ds(0, both),
        )
        td_ref[i, 0] = d_k
        td_ref[i, 1] = d_v

        for d in range(2):
            @pl.when(side_on[d])
            def _(d=d):
                @pl.loop(0, 3)
                def _(row):
                    @pl.when(row_on(row))
                    def _():
                        bwd(i, row, 3 * d, pl.ds(d * bq, bq), p_side[row, d])
                        g1(i, row, d).start()

        @pl.when(i > 0)
        def _():
            add_g2(i - 1)

        @pl.loop(0, 6)
        def _(n):
            row = n // 2
            col = 1 + n % 2

            @pl.when(row_on(row))
            def _():
                bwd(i, row, col, pl.ds(0, both), p_mid[row, col - 1])

        fin[i, 1] = (dq_t[...] * scale).T.astype(BF16)
        g3(i, 1).start()
        local_out(i, 1).start()

    add_g1(nh - 1)
    add_g2(nh - 1)

    mask_out.wait_send()

    @pl.loop(0, nh)
    def _(i):
        for j in range(4):
            r1(i, j).wait_send()
            g3(i, j).wait_send()
            g3(i, j).wait_recv()
            local_out(i, j).wait()
        for d in range(2):
            @pl.when(vert_on[d])
            def _(d=d):
                r2(i, d).wait_send()
                g2(i, d).wait_send()
        for_sides(i, (0, 1, 2), lambda i, r, d: r3(i, r, d).wait_send(), False)
        for_sides(i, (0, 1, 2), lambda i, r, d: g1(i, r, d).wait_send(), False)


def window_pass(query, key, value, grad, mask, text_key, text_value, text_mask):
    nx = lax.axis_size("tm") // 2
    ny = lax.axis_size("height") // 2
    bq, channels = query.shape
    nh = channels // HD // 2
    words = text_key.shape[0]
    both = 2 * bq
    sds = jax.ShapeDtypeStruct
    hbm = pl.BlockSpec(memory_space=pl.ANY)
    vmem = pl.BlockSpec(memory_space=pltpu.VMEM)
    dma = pltpu.SemaphoreType.DMA
    return pl.pallas_call(
        functools.partial(window_kernel, nx, ny),
        out_shape=[sds((bq, channels), BF16)] * 4 + [sds((nh, 2, words, HD), F32)],
        in_specs=[hbm, hbm, hbm, hbm, vmem, vmem, vmem, vmem],
        out_specs=[hbm] * 4 + [vmem],
        scratch_shapes=[
            pltpu.VMEM((nh, 2, 3, 4, bq, HD), BF16),
            pltpu.VMEM((nh, 2, both, HD), BF16),
            pltpu.VMEM((24, both), F32),
            pltpu.VMEM((3, 2, bq, both), BF16),
            pltpu.VMEM((3, 2, bq, bq), BF16),
            pltpu.VMEM((words, both), BF16),
            pltpu.VMEM((16, both), F32),
            pltpu.VMEM((8, both), F32),
            pltpu.VMEM((8, both), F32),
            pltpu.VMEM((8, both), F32),
            pltpu.VMEM((HD, both), F32),
            pltpu.VMEM((HD, both), F32),
            pltpu.VMEM((nh, 2, 3, 4, bq, HD), BF16),
            pltpu.VMEM((nh, 2, 2, 3, bq, HD), BF16),
            pltpu.VMEM((nh, 2, 2, 2, bq, HD), BF16),
            pltpu.VMEM((nh, 4, both, HD), BF16),
            dma((nh, 4)),
            dma((nh, 4)),
            dma((nh, 4)),
            dma((3,)),
            dma((nh, 2)),
            dma((nh, 2)),
            dma((nh, 3, 2)),
            dma((nh, 3, 2)),
            dma((nh, 3, 2)),
            dma((nh, 3, 2)),
            dma((nh, 2)),
            dma((nh, 2)),
            dma((nh, 4)),
            dma((nh, 4)),
            dma((nh, 4)),
        ],
        compiler_params=pltpu.CompilerParams(
            collective_id=0, has_side_effects=True, vmem_limit_bytes=62 * 2**20
        ),
        name="window",
    )(query, key, value, grad, mask, text_key, text_value, text_mask)


def edge_mask(tile_lists, tile, slot):
    lists = tile_lists.reshape(4, 3, 3, 3)
    rows = []
    for col in (0, 3):
        on = jnp.any((lists >= 0) & (lists % 4 == col), axis=-1)
        rows.append(on)
    on = jnp.stack(rows, -1)
    on = jnp.transpose(on, (1, 2, 3, 0)).reshape(18, 4).astype(F32)
    on = jnp.repeat(on, tile, axis=1)
    pad = jnp.zeros((6, on.shape[1]), F32)
    return jnp.where(
        slot == 0, jnp.concatenate([on, pad]), jnp.concatenate([pad, on])
    )


def body(
    query_latent,
    key_latent,
    value_latent,
    grad_latent,
    tile_lists,
    text_query,
    text_key,
    text_value,
    grad_text,
    text_mask,
):
    frames, rows, width_tiles, tile, channels = query_latent.shape
    head_dim = HD
    heads = channels // head_dim
    nh = heads // 2
    score_scale = 1.0 / math.sqrt(head_dim)
    text_on = text_mask > 0
    key_text = text_key.reshape(-1, heads, head_dim)
    value_text = text_value.reshape(-1, heads, head_dim)
    query_text = text_query.reshape(-1, heads, head_dim)
    grad_words = grad_text.reshape(-1, heads, head_dim)
    t = lax.axis_index("tm")
    h = lax.axis_index("height")
    half = (t % 2 + h // (lax.axis_size("height") // 2)) % 2
    flat = [
        a.reshape(width_tiles * tile, channels)
        for a in (query_latent, key_latent, value_latent, grad_latent)
    ]
    mask = edge_mask(tile_lists, tile, t % 2)
    tm_cols = jnp.broadcast_to(text_on.astype(F32)[:, None], (text_on.shape[0], HD))
    out_latent, grad_q_latent, win_dk, win_dv, td = window_pass(
        *flat, mask, text_key, text_value, tm_cols
    )
    td = jnp.transpose(td, (1, 2, 0, 3)).reshape(2, -1, nh * head_dim)
    wide = jnp.zeros((2, td.shape[1], channels), F32)
    wide = lax.dynamic_update_slice(
        wide, td, (jnp.int32(0), jnp.int32(0), (half * nh * head_dim).astype(jnp.int32))
    )
    text_dk, text_dv = wide[0], wide[1]

    own_keys = key_latent.reshape(-1, heads, head_dim)
    own_values = value_latent.reshape(-1, heads, head_dim)
    score_own = (
        jnp.einsum("ihd,jhd->hij", query_text, own_keys, preferred_element_type=F32) * score_scale
    )
    score_words = (
        jnp.einsum("ihd,jhd->hij", query_text, key_text, preferred_element_type=F32) * score_scale
    )
    score_words = jnp.where(text_on[None, None, :], score_words, -jnp.inf)
    local_peak = jnp.max(score_own, -1)
    peak = lax.pmax(local_peak, ("tm", "height"))
    peak = jnp.maximum(peak, jnp.max(score_words, -1))
    local_total = jnp.sum(jnp.exp(score_own - peak[..., None]), -1)
    total = lax.psum(local_total, ("tm", "height"))
    total = total + jnp.sum(jnp.exp(score_words - peak[..., None]), -1)
    log_total = (peak + jnp.log(total))[..., None]
    prob_own = jnp.exp(score_own - log_total)
    prob_words = jnp.exp(score_words - log_total)
    weight_own = prob_own.astype(BF16)
    weight_words = prob_words.astype(BF16)
    numer = jnp.einsum(
        "hij,jhd->ihd", weight_own, own_values, preferred_element_type=F32
    ).reshape(-1, channels)
    numer = lax.psum(numer, ("tm", "height"))
    words_part = jnp.einsum(
        "hij,jhd->ihd", weight_words, value_text, preferred_element_type=F32
    ).reshape(-1, channels)
    out_text = (numer + words_part).astype(BF16)
    row_delta = jnp.transpose(
        jnp.sum(grad_words.astype(F32) * out_text.reshape(-1, heads, head_dim).astype(F32), -1),
        (1, 0),
    )[..., None]
    dscore_own = (
        prob_own
        * (
            jnp.einsum("ihd,jhd->hij", grad_words, own_values, preferred_element_type=F32)
            - row_delta
        )
    ).astype(BF16)
    dscore_words = (
        prob_words
        * (
            jnp.einsum("ihd,jhd->hij", grad_words, value_text, preferred_element_type=F32)
            - row_delta
        )
    ).astype(BF16)
    query_part = (
        jnp.einsum("hij,jhd->ihd", dscore_own, own_keys, preferred_element_type=F32) * score_scale
    )
    own_dk = (
        jnp.einsum("hij,ihd->jhd", dscore_own, query_text, preferred_element_type=F32)
        * score_scale
    )
    own_dv = jnp.einsum("hij,ihd->jhd", weight_own, grad_words, preferred_element_type=F32)
    summed_q, summed_k, summed_v = lax.psum(
        (query_part.reshape(-1, channels), text_dk, text_dv), ("tm", "height")
    )
    words_q = (
        jnp.einsum("hij,jhd->ihd", dscore_words, key_text, preferred_element_type=F32)
        * score_scale
    )
    words_k = (
        jnp.einsum("hij,ihd->jhd", dscore_words, query_text, preferred_element_type=F32)
        * score_scale
    )
    words_v = jnp.einsum("hij,ihd->jhd", weight_words, grad_words, preferred_element_type=F32)
    grad_q_text = (summed_q + words_q.reshape(-1, channels)).astype(BF16)
    grad_k_text = (summed_k + words_k.reshape(-1, channels)).astype(BF16)
    grad_v_text = (summed_v + words_v.reshape(-1, channels)).astype(BF16)
    shape = query_latent.shape
    grad_k_latent = (win_dk.astype(F32) + own_dk.reshape(win_dk.shape)).astype(BF16)
    grad_v_latent = (win_dv.astype(F32) + own_dv.reshape(win_dv.shape)).astype(BF16)
    return (
        out_latent.reshape(shape),
        grad_q_latent.reshape(shape),
        grad_k_latent.reshape(shape),
        grad_v_latent.reshape(shape),
        out_text,
        grad_q_text,
        grad_k_text,
        grad_v_text,
    )


def solution(mesh):
    latent = P("tm", "height", None, None, "heads")
    text = P(None, "heads")
    in_specs = (latent,) * 4 + (P("tm", "height", None, None),) + (text,) * 4 + (P(),)
    out_specs = (latent,) * 4 + (text,) * 4
    return jax.shard_map(body, mesh=mesh, in_specs=in_specs, out_specs=out_specs, check_vma=False)
```

time: 1180 us -> 684 us (0.58)
  waiting for transfers between devices: 395 us -> 113 us
  Pallas kernels: 0 us -> 138 us
  matrix products: 147 us -> 18.2 us
  local copies, waits for them, and re-layouts: 120 us -> 29.6 us
  other arithmetic: 64.7 us -> 13.6 us
  blocking collectives: 406 us -> 356 us
  starting transfers between devices: 27.1 us -> 0.08 us
    ppermute x8 -> x0, waiting for transfers between devices: 164 us -> none  [the longest x2 129 us: extended(): lax.ppermute(lax.slice_in_dim(block, 0, width, axis=dim), axis, backward)]
    pallas_call x0 -> x1, Pallas kernels: none -> 138 us  [window_pass(): pl.pallas_call(functools.partial(window_kernel, nx, ny), out_shape=[sds((...]
    dot_general x75 -> x3, matrix products: 131 us -> 4.78 us  [the longest x1 1.83 us: body(): jnp.einsum('ihd,jhd->hij', query_text, own_keys, preferred_element_type=F32)]
    psum x1, waiting for transfers between devices: 106 us -> 0.01 us  [body(): numer = lax.psum(numer, ('tm', 'height'))]
    pmax x1, blocking collectives: 230 us -> 183 us  [body(): peak = lax.pmax(local_peak, ('tm', 'height'))]
    slice x6 -> x0, local copies, waits for them, and re-layouts: 34.7 us -> none  [one_head(): value_head = cut(nearby[1])]
    ppermute x8 -> x0, starting transfers between devices: 27 us -> none  [the longest x4 13 us: from_behind(): return lax.ppermute(block, axis, route)]
    while x84 -> x0, local copies, waits for them, and re-layouts: 22.1 us -> none
  transfers between devices with their start and end apart: 10 -> 2, of which waited for: 6 -> 1; matrix products, arithmetic and copies ran while one was open for 7% -> 5% of each run, Pallas kernels for 0% -> 20%
where the time goes in v1:
time: 684 us; the launch traced here: 683 us
  blocking collectives  356 us (52%)
  Pallas kernels  138 us (20%)
  waiting for transfers between devices  113 us (17%)
  local copies, waits for them, and re-layouts  29.6 us (4%)
  matrix products  18.2 us (3%)
  between operations  14.5 us (2%)
  other arithmetic  13.6 us (2%)
    pmax x1, blocking collectives, body(): peak = lax.pmax(local_peak, ('tm', 'height'))  183 us
    psum x1, blocking collectives, body(): total = lax.psum(local_total, ('tm', 'height'))  174 us
    pallas_call x1, Pallas kernels, window_pass(): pl.pallas_call(functools.partial(window_kernel, nx, ny), out_shape=[sds((...  138 us
    psum x1, waiting for transfers between devices, body(): lax.psum((query_part.reshape(-1, channels), text_dk, text_dv), ('tm', 'he...  113 us
  transfers between devices with their start and end apart: 2, of which 1 were waited for; matrix products, arithmetic and copies ran while one was open for 5% of the time, Pallas kernels for 20%

profile of v1, /device:TPU:0, one launch (start us, length us, event | category | flops | bytes accessed | tf_op | source)
XLA Modules:
  0.0 683.0 jit_solution(3513005520467019461)
XLA Ops:
  7.2 1.3 fusion.15
  9.7 2.1 copy.84
  15.3 1.8 multiply_reduce_fusion
  17.2 182.6 %pmax.7 = f32[6,256]{1,0:T(8,128)S(1)} all-reduce(f32[6,256]{1,0:T(8,128)S(1)} %get-tuple-element.43), channel_id=1, replica_groups=mesh['tm'=8,'height'=8,'heads'=2] {'tm','height'}, use_global_device_ids=true, to_apply=%region_3.4 | all-reduce | flops 1536 | bytes 12288 | tf_op jit(solution)/shard_map/pmax | solution.py:606
  199.7 1.4 fusion.16
  203.5 173.8 %psum.35 = f32[6,256]{1,0:T(8,128)S(1)} all-reduce(f32[6,256]{1,0:T(8,128)S(1)} %exponential_reduce_fusion), channel_id=1, replica_groups=mesh['tm'=8,'height'=8,'heads'=2] {'tm','height'}, use_global_device_ids=true, to_apply=%region_6.7 | all-reduce | flops 1536 | bytes 12288 | tf_op jit(solution)/shard_map/psum | solution.py:609
  377.3 2.9 fusion.6
  384.7 137.8 %window.1 = (bf16[512,768]{1,0:T(8,128)(2,1)}, bf16[512,768]{1,0:T(8,128)(2,1)}, bf16[512,768]{1,0:T(8,128)(2,1)}, bf16[512,768]{1,0:T(8,128)(2,1)}, f32[3,2,256,128]{3,2,1,0:T(8,128)}) custom-call(bf16[512,768]{1,0:T(8,128)(2,1)} %bitcast.110, bf16[512,768]{1,0:T(8,128)(2,1)} %bitcast.103, bf16[512,768]{1,0:T(8,128)(2,1)} %bitcast.104, ...), custom_call_target="tpu_custom_call" | custom-call | tf_op jit(solution)/shard_map/window/pallas_call | solution.py:495
  522.5 1.4 copy.101
  524.4 1.3 slice_bitcast_fusion
  527.7 1.5 fusion.3
  531.2 1.5 convolution_multiply_fusion.3
  532.7 2.3 copy.95
  535.0 2.7 fusion.8
  537.7 2.3 copy.106
  540.0 1.9 fusion.4
  541.9 1.9 copy.94
  543.8 2.3 add_convert_fusion
  546.1 1.9 copy.107
  548.1 1.5 multiply_convert_fusion.1
  552.3 2.3 copy.100
  555.5 2.2 add_convert_fusion.1
  557.7 112.9 %all-reduce.8.cloned.1.call-done = (f32[256,768]{1,0:T(8,128)}, f32[256,768]{1,0:T(8,128)}, f32[256,768]{1,0:T(8,128)}) async-done(((f32[256,768]{1,0:T(8,128)}, f32[256,768]{1,0:T(8,128)}, f32[256,768]{1,0:T(8,128)}), (f32[256,768]{1,0:T(8,128)}, f32[256,768]{1,0:T(8,128)}, f32[256,768]{1,0:T(8,128)})) %all-reduce.8.cloned.1.call-update) | async-done | bytes 2359312 | tf_op jit(solution)/shard_map/psum | solution.py:650
  670.6 2.1 add_convert_fusion.2
  (94 shorter events, 22.8 us)
Async XLA Ops:
  7.2 4.6 copy-start.17
  7.2 520.5 %all-reduce.6.cloned.1.call-start = ((), (), s32[]{:S(2)}) async-start(), calls=%async_computation | async-start | bytes 1572864 | tf_op jit(solution)/shard_map/psum | solution.py:619
  9.7 190.0 %copy-start.7 = (bf16[256,768]{0,1:T(8,128)(2,1)}, bf16[256,768]{0,1:T(8,128)(2,1)S(1)}, u32[]{:S(2)}) copy-start(bf16[256,768]{0,1:T(8,128)(2,1)S(1)} %copy.80) | copy-start | bytes 1179652
  11.8 1.8 copy-start.18
  17.2 360.1 %copy-start = (f32[6,256,512]{2,1,0:T(8,128)}, f32[6,256,512]{2,1,0:T(8,128)S(1)}, u32[]{:S(2)}) copy-start(f32[6,256,512]{2,1,0:T(8,128)S(1)} %get-tuple-element.44) | copy-start | bytes 9437188
  377.3 3.0 copy-start.25
  380.2 2.2 copy-start.19
  380.2 3.8 copy-start.24
  380.3 290.4 %all-reduce.8.cloned.1.call-start = ((), (), s32[]{:S(2)}) async-start(), calls=%async_computation.1 | async-start | bytes 4718592 | tf_op jit(solution)/shard_map/psum | solution.py:650
  524.4 2.0 copy-start.3
  524.4 2.0 copy-start.11
  526.4 3.6 copy-start.1
  527.7 2.3 copy-start.9
  531.1 1.5 copy-start.5
  543.8 4.2 copy-start.4
  549.6 1.6 copy-start.13
  551.2 3.5 copy-start.6
  555.5 115.2 %copy-start.14 = (f32[256,768]{1,0:T(8,128)S(1)}, f32[256,768]{1,0:T(8,128)}, u32[]{:S(2)}) copy-start(f32[256,768]{1,0:T(8,128)} %copy.106) | copy-start | bytes 2359300
  557.7 115.0 %copy-start.16 = (f32[256,768]{1,0:T(8,128)S(1)}, f32[256,768]{1,0:T(8,128)}, u32[]{:S(2)}) copy-start(f32[256,768]{1,0:T(8,128)} %copy.100) | copy-start | bytes 2359300
  670.6 2.1 copy-start.23
  670.6 2.9 copy-start.15
  670.6 2.9 copy-start.22
  672.8 1.7 copy-start.21
  673.6 1.7 copy-start.20
  (4 other events, 4.6 us)
Sparse Core Ops, SparseCore 0:
  380.4 126.3 all-reduce.5
  535.1 135.4 all-reduce.7

commit v2 on v1

--- a/solution.py
+++ b/solution.py
@@ -35,14 +35,19 @@
     v_ref,
     g_ref,
     mask_ref,
+    tq_ref,
     tk_ref,
     tv_ref,
+    tg_ref,
     tm_ref,
     out_ref,
     dq_ref,
     dk_ref,
     dv_ref,
-    td_ref,
+    tout_ref,
+    tdq_ref,
+    tdk_ref,
+    tdv_ref,
     kv,
     qg,
     mask,
@@ -59,6 +64,16 @@
     g1r,
     g2r,
     fin,
+    st,
+    st_in,
+    lse,
+    part,
+    from_z,
+    from_y,
+    from_x,
+    whole,
+    t_kv,
+    t_fin,
     sem_loc,
     sem_r1s,
     sem_r1r,
@@ -74,6 +89,13 @@
     sem_g3s,
     sem_g3r,
     sem_out,
+    sem_sts,
+    sem_str,
+    sem_ars,
+    sem_arr,
+    sem_tfs,
+    sem_tfr,
+    sem_tfl,
 ):
     bq = q_ref.shape[0]
     tile = bq // 4
@@ -106,30 +128,27 @@
     has_up = h > 0
     has_down = h < rows_all - 1
 
+    y = h % ny
+    words_n = tq_ref.shape[0]
+    lanes = words_n // HD
+    z_peer = (2 * x + (half + 1 - zh) % 2, (1 - zh) * ny + y, c)
+    y_peers = [(t, zh * ny + (y + p) % ny, c) for p in range(1, ny)]
+    x_peers = [(2 * ((x + p) % nx) + zl, h, c) for p in range(1, nx)]
+    cross_up = h == ny
+    cross_down = h == ny - 1
+
     barrier = pltpu.get_barrier_semaphore()
-    greet = [
-        (None, partner),
-        (has_left, left),
-        (has_right, right),
-        (has_up, up),
-        (has_down, down),
-    ]
-    for cond, dev in greet:
-        def hello(dev=dev):
+    for dev in [partner, z_peer] + y_peers + x_peers:
+        pl.semaphore_signal(barrier, inc=1, device_id=dev, device_id_type=MESH)
+    for cond, dev in ((cross_up, up), (cross_down, down)):
+        @pl.when(cond)
+        def _(dev=dev):
             pl.semaphore_signal(barrier, inc=1, device_id=dev, device_id_type=MESH)
 
-        if cond is None:
-            hello()
-        else:
-            pl.when(cond)(hello)
-    count = (
-        1
-        + has_left.astype(jnp.int32)
-        + has_right.astype(jnp.int32)
-        + has_up.astype(jnp.int32)
-        + has_down.astype(jnp.int32)
+    pl.semaphore_wait(
+        barrier,
+        nx + ny + cross_up.astype(jnp.int32) + cross_down.astype(jnp.int32),
     )
-    pl.semaphore_wait(barrier, count)
 
     def remote(src, dst, ssem, rsem, dev):
         return pltpu.make_async_remote_copy(
@@ -235,6 +254,202 @@
     def wait_r3(i):
         for_sides(i, (0, 1, 2), lambda i, r, d: r3(i, r, d).wait_recv(), True)
 
+    first = (x == 0) & (h == 0)
+    half_rows = part.shape[1] // 2
+    quarter = half_rows // ny
+    piece = quarter // nx
+    z_at = zh * half_rows
+    y_at = z_at + y * quarter
+    x_at = y_at + x * piece
+    round_y = [(j, y_peers[j], (y + j + 1) % ny) for j in range(ny - 1)]
+    round_x = [(j, x_peers[j], (x + j + 1) % nx) for j in range(nx - 1)]
+    n_y, n_x = ny - 1, nx - 1
+
+    def rows8(at, n):
+        return pl.ds(pl.multiple_of(at, 8), n)
+
+    def ar(n, src, dst, k, dev):
+        return remote(src, dst, sem_ars.at[n, k], sem_arr.at[n, k], dev)
+
+    def ar_copies(n, step):
+        if step == 0:
+            return [ar(n, part.at[n, rows8((1 - zh) * half_rows, half_rows)], from_z.at[n], 0, z_peer)]
+        if step == 1:
+            return [
+                ar(n, part.at[n, rows8(z_at + to * quarter, quarter)], from_y.at[n, j], 1 + j, dev)
+                for j, dev, to in round_y
+            ]
+        if step == 2:
+            return [
+                ar(n, part.at[n, rows8(y_at + to * piece, piece)], from_x.at[n, j], 1 + n_y + j, dev)
+                for j, dev, to in round_x
+            ]
+        if step == 3:
+            mine = whole.at[n, rows8(x_at, piece)]
+            return [ar(n, mine, mine, 1 + n_y + n_x + j, dev) for j, dev, _ in round_x]
+        if step == 4:
+            mine = whole.at[n, rows8(y_at, quarter)]
+            return [ar(n, mine, mine, 1 + n_y + 2 * n_x + j, dev) for j, dev, _ in round_y]
+        mine = whole.at[n, rows8(z_at, half_rows)]
+        return [ar(n, mine, mine, 1 + 2 * n_y + 2 * n_x, z_peer)]
+
+    def ar_step(n, step):
+        if step > 0:
+            for copy in ar_copies(n, step - 1):
+                copy.wait_recv()
+        if step == 1:
+            part[n, rows8(z_at, half_rows)] += from_z[n]
+        if step == 2:
+            at = rows8(y_at, quarter)
+            total = part[n, at]
+            for j in range(n_y):
+                total = total + from_y[n, j]
+            part[n, at] = total
+        if step == 3:
+            at = rows8(x_at, piece)
+            total = part[n, at]
+            for j in range(n_x):
+                total = total + from_x[n, j]
+            whole[n, at] = total
+        if step < 6:
+            for copy in ar_copies(n, step):
+                copy.start()
+
+    def st_copies(step):
+        if step == 0:
+            peers, base = [z_peer], 0
+        elif step == 1:
+            peers, base = y_peers, 1
+        else:
+            peers, base = x_peers, 1 + n_y
+        return [
+            remote(st.at[step], st_in.at[base + j], sem_sts.at[base + j], sem_str.at[base + j], dev)
+            for j, dev in enumerate(peers)
+        ], base
+
+    def st_start(step):
+        for copy in st_copies(step)[0]:
+            copy.start()
+
+    def st_merge(step):
+        copies, base = st_copies(step)
+        for copy in copies:
+            copy.wait_recv()
+        own = st[step]
+        peak = own[0:nh]
+        for j in range(len(copies)):
+            peak = jnp.maximum(peak, st_in[base + j][0:nh])
+        total = own[nh : 2 * nh] * jnp.exp2(own[0:nh] - peak)
+        for j in range(len(copies)):
+            got = st_in[base + j]
+            total = total + got[nh : 2 * nh] * jnp.exp2(got[0:nh] - peak)
+        st[step + 1, 0:nh] = peak
+        st[step + 1, nh : 2 * nh] = total
+
+    def text_scores(i):
+        keys = kv[i, 0, 1, 1:3].reshape(both, HD)
+        return mm_nt(keys, tq_ref[:, head_cols(half, i)]) * c2
+
+    def words_scores(i):
+        cols = head_cols(half, i)
+        s = mm_nt(tk_ref[:, cols], tq_ref[:, cols]) * c2
+        return jnp.where(tm_ref[:, 0:1] > 0.5, s, NEG)
+
+    def text_stats(i):
+        s = text_scores(i)
+        peak = jnp.max(s, 0, keepdims=True)
+        st[0, pl.ds(i, 1)] = peak
+        st[0, pl.ds(nh + i, 1)] = jnp.sum(jnp.exp2(s - peak), 0, keepdims=True)
+
+        @pl.when(first)
+        def _():
+            s2 = words_scores(i)
+            old = st[0, pl.ds(i, 1)]
+            new = jnp.maximum(old, jnp.max(s2, 0, keepdims=True))
+            st[0, pl.ds(i, 1)] = new
+            st[0, pl.ds(nh + i, 1)] = st[0, pl.ds(nh + i, 1)] * jnp.exp2(old - new) + jnp.sum(
+                jnp.exp2(s2 - new), 0, keepdims=True
+            )
+
+    def put_t(n, i, value):
+        for a in range(lanes):
+            part[n, rows8(i * words_n + a * HD, HD)] = value[:, a * HD : (a + 1) * HD]
+
+    def add_t(n, i, value):
+        for a in range(lanes):
+            part[n, rows8(i * words_n + a * HD, HD)] += value[:, a * HD : (a + 1) * HD]
+
+    def get_t(n, i):
+        return jnp.concatenate(
+            [whole[n, rows8(i * words_n + a * HD, HD)] for a in range(lanes)], axis=1
+        )
+
+    def text_forward(i):
+        row = lse[pl.ds(i, 1)]
+        w = jnp.exp2(text_scores(i) - row).astype(BF16)
+        put_t(0, i, mm_tn(kv[i, 1, 1, 1:3].reshape(both, HD), w))
+
+        @pl.when(first)
+        def _():
+            w2 = jnp.exp2(words_scores(i) - row).astype(BF16)
+            add_t(0, i, mm_tn(tv_ref[:, head_cols(half, i)], w2))
+
+    def td_at(i, a):
+        at = 2 * i + a
+        return (2 + at // nh, rows8((at % nh) * words_n, words_n))
+
+    def text_backward(i):
+        cols = head_cols(half, i)
+        row = lse[pl.ds(i, 1)]
+        q = tq_ref[:, cols]
+        g = tg_ref[:, cols]
+        o_round = get_t(0, i).astype(BF16).astype(F32)
+        t_fin[0, i] = o_round.T.astype(BF16)
+        delta = jnp.sum(o_round * g.astype(F32).T, 0, keepdims=True)
+
+        def one(s, k, v):
+            p = jnp.exp2(s - row)
+            ds = (p * (mm_nt(v, g) - delta)).astype(BF16)
+            return mm_tn(k, ds), mm_nn(ds, q) * scale, mm_nn(p.astype(BF16), g)
+
+        a_q, a_k, a_v = one(
+            text_scores(i), kv[i, 0, 1, 1:3].reshape(both, HD), kv[i, 1, 1, 1:3].reshape(both, HD)
+        )
+        put_t(1, i, a_q)
+        t_kv[i, 0] = a_k
+        t_kv[i, 1] = a_v
+
+        @pl.when(first)
+        def _():
+            b_q, b_k, b_v = one(words_scores(i), tk_ref[:, cols], tv_ref[:, cols])
+            add_t(1, i, b_q)
+            n, at = td_at(i, 0)
+            part[n, at] += b_k
+            n, at = td_at(i, 1)
+            part[n, at] += b_v
+
+    t_outs = (tout_ref, tdq_ref, tdk_ref, tdv_ref)
+
+    def t_out(j, i):
+        return remote(
+            t_fin.at[j, i], t_outs[j].at[:, head_cols(half, i)],
+            sem_tfs.at[j, i], sem_tfr.at[j, i], partner,
+        )
+
+    def t_loc(j, i):
+        return pltpu.make_async_copy(
+            t_fin.at[j, i], t_outs[j].at[:, head_cols(half, i)], sem_tfl.at[j, i]
+        )
+
+    def send_text(j, i):
+        t_out(j, i).start()
+        t_loc(j, i).start()
+
+    def finish_td(i, a):
+        n, at = td_at(i, a)
+        t_fin[2 + a, i] = whole[n, at].astype(BF16)
+        send_text(2 + a, i)
+
     @pl.loop(0, nh)
     def _(i):
         for j in range(4):
@@ -264,9 +479,13 @@
 
     mask_own.wait()
     mask_out.wait_recv()
+    part[2] = jnp.zeros(part.shape[1:], F32)
+    part[3] = jnp.zeros(part.shape[1:], F32)
+    st[0] = jnp.zeros(st.shape[1:], F32)
     wait_r1(0)
     start_r2(0)
     start_r3(0, (1,))
+    text_stats(0)
 
     def online(s, v, save, qs, keep):
         m_old = m_run[0:1, qs]
@@ -349,6 +568,7 @@
                     + g1r[i, 1 - s, a, 1].astype(F32)
                     + g2r[i, 0, a, s].astype(F32)
                     + g2r[i, 1, a, s].astype(F32)
+                    + t_kv[i, a, s * bq : (s + 1) * bq]
                 )
                 fin[i, 2 + a, s * bq : (s + 1) * bq] = total.astype(BF16)
         for j in (2, 3):
@@ -362,15 +582,29 @@
         o_t[...] = jnp.zeros(o_t.shape, F32)
         dq_t[...] = jnp.zeros(dq_t.shape, F32)
 
+        @pl.when(i == 1)
+        def _():
+            @pl.loop(0, nh)
+            def _(j):
+                text_backward(j)
+                send_text(0, j)
+
+            ar_step(1, 0)
+
         @pl.loop(1, 3)
         def _(col):
             fwd_mid(i, 1, col)
 
+        @pl.when(i == 1)
+        def _():
+            ar_step(1, 1)
+
         @pl.when(i == 0)
         def _():
             wait_r1(1)
             start_r2(1)
             start_r3(1, (1,))
+            text_stats(1)
             wait_r2(0)
             start_r3(0, (0, 2))
 
@@ -387,6 +621,12 @@
             wait_r1(2)
             start_r2(2)
             start_r3(2, (1,))
+            text_stats(2)
+            st_start(0)
+
+        @pl.when(i == 1)
+        def _():
+            ar_step(1, 2)
 
         @pl.when(i < nh - 1)
         def _():
@@ -406,6 +646,15 @@
         @pl.when(i > 0)
         def _():
             add_g1(i - 1)
+
+        @pl.when(i == 0)
+        def _():
+            st_merge(0)
+            st_start(1)
+
+        @pl.when(i == 1)
+        def _():
+            ar_step(1, 3)
 
         wait_r3(i)
         for d in range(2):
@@ -417,6 +666,33 @@
                     def _():
                         fwd_side(i, row, d)
 
+            @pl.when(i == 0)
+            def _(d=d):
+                st_merge(d + 1)
+                if d == 0:
+                    st_start(2)
+
+            @pl.when(i == 1)
+            def _(d=d):
+                ar_step(1, 4 + d)
+
+        @pl.when(i == 0)
+        def _():
+            lse[0:nh] = st[3, 0:nh] + jnp.log2(st[3, nh : 2 * nh])
+
+            @pl.loop(0, nh)
+            def _(j):
+                text_forward(j)
+
+        @pl.when(i == 1)
+        def _():
+            ar_step(1, 6)
+
+            @pl.loop(0, nh)
+            def _(j):
+                t_fin[1, j] = (get_t(1, j) * scale).T.astype(BF16)
+                send_text(1, j)
+
         inv = 1.0 / l_run[0:1, :]
         l_run[0:1, :] = inv
         o_round = (o_t[...] * inv).astype(BF16).astype(F32)
@@ -430,8 +706,12 @@
             p_text[...], tk_ref[:, words], tv_ref[:, words], qg[i, 0], qg[i, 1],
             12, pl.ds(0, both),
         )
-        td_ref[i, 0] = d_k
-        td_ref[i, 1] = d_v
+        n, at = td_at(i, 0)
+        part[n, at] += d_k
+        n, at = td_at(i, 1)
+        part[n, at] += d_v
+        turn = jnp.where(i == 0, 0, i + 1)
+        ar_step(turn, 0)
 
         for d in range(2):
             @pl.when(side_on[d])
@@ -443,25 +723,52 @@
                         bwd(i, row, 3 * d, pl.ds(d * bq, bq), p_side[row, d])
                         g1(i, row, d).start()
 
+            ar_step(turn, 1 + d)
+
         @pl.when(i > 0)
         def _():
             add_g2(i - 1)
 
-        @pl.loop(0, 6)
-        def _(n):
-            row = n // 2
-            col = 1 + n % 2
-
+        for stage, row in enumerate((0, 2, 1)):
             @pl.when(row_on(row))
-            def _():
-                bwd(i, row, col, pl.ds(0, both), p_mid[row, col - 1])
+            def _(row=row):
+                @pl.loop(1, 3)
+                def _(col):
+                    bwd(i, row, col, pl.ds(0, both), p_mid[row, col - 1])
+
+            ar_step(turn, 3 + stage)
 
         fin[i, 1] = (dq_t[...] * scale).T.astype(BF16)
         g3(i, 1).start()
         local_out(i, 1).start()
 
+        @pl.when(i < nh - 1)
+        def _():
+            ar_step(turn, 6)
+
     add_g1(nh - 1)
+    for at in range(nh):
+        finish_td(at // 2, at % 2)
+    ar_step(3, 6)
+    for at in range(nh, 2 * nh):
+        finish_td(at // 2, at % 2)
     add_g2(nh - 1)
+
+    for step in range(3):
+        for copy in st_copies(step)[0]:
+            copy.wait_send()
+
+    @pl.loop(0, 4)
+    def _(n):
+        for step in range(6):
+            for copy in ar_copies(n, step):
+                copy.wait_send()
+
+    for n in range(4):
+        for j in range(nh):
+            t_out(n, j).wait_send()
+            t_out(n, j).wait_recv()
+            t_loc(n, j).wait()
 
     mask_out.wait_send()
 
@@ -481,22 +788,25 @@
         for_sides(i, (0, 1, 2), lambda i, r, d: g1(i, r, d).wait_send(), False)
 
 
-def window_pass(query, key, value, grad, mask, text_key, text_value, text_mask):
+def window_pass(
+    query, key, value, grad, mask, text_query, text_key, text_value, text_grad, text_mask
+):
     nx = lax.axis_size("tm") // 2
     ny = lax.axis_size("height") // 2
     bq, channels = query.shape
     nh = channels // HD // 2
     words = text_key.shape[0]
     both = 2 * bq
+    rows = nh * words
     sds = jax.ShapeDtypeStruct
     hbm = pl.BlockSpec(memory_space=pl.ANY)
     vmem = pl.BlockSpec(memory_space=pltpu.VMEM)
     dma = pltpu.SemaphoreType.DMA
     return pl.pallas_call(
         functools.partial(window_kernel, nx, ny),
-        out_shape=[sds((bq, channels), BF16)] * 4 + [sds((nh, 2, words, HD), F32)],
-        in_specs=[hbm, hbm, hbm, hbm, vmem, vmem, vmem, vmem],
-        out_specs=[hbm] * 4 + [vmem],
+        out_shape=[sds((bq, channels), BF16)] * 4 + [sds((words, channels), BF16)] * 4,
+        in_specs=[hbm] * 4 + [vmem] * 6,
+        out_specs=[hbm] * 8,
         scratch_shapes=[
             pltpu.VMEM((nh, 2, 3, 4, bq, HD), BF16),
             pltpu.VMEM((nh, 2, both, HD), BF16),
@@ -514,6 +824,16 @@
             pltpu.VMEM((nh, 2, 2, 3, bq, HD), BF16),
             pltpu.VMEM((nh, 2, 2, 2, bq, HD), BF16),
             pltpu.VMEM((nh, 4, both, HD), BF16),
+            pltpu.VMEM((4, 8, words), F32),
+            pltpu.VMEM((nx + ny - 1, 8, words), F32),
+            pltpu.VMEM((8, words), F32),
+            pltpu.VMEM((4, rows, HD), F32),
+            pltpu.VMEM((4, rows // 2, HD), F32),
+            pltpu.VMEM((4, ny - 1, rows // 2 // ny, HD), F32),
+            pltpu.VMEM((4, nx - 1, rows // 2 // ny // nx, HD), F32),
+            pltpu.VMEM((4, rows, HD), F32),
+            pltpu.VMEM((nh, 2, both, HD), F32),
+            pltpu.VMEM((4, nh, words, HD), BF16),
             dma((nh, 4)),
             dma((nh, 4)),
             dma((nh, 4)),
@@ -529,12 +849,19 @@
             dma((nh, 4)),
             dma((nh, 4)),
             dma((nh, 4)),
+            dma((nx + ny - 1,)),
+            dma((nx + ny - 1,)),
+            dma((4, 2 * (nx + ny - 1))),
+            dma((4, 2 * (nx + ny - 1))),
+            dma((4, nh)),
+            dma((4, nh)),
+            dma((4, nh)),
         ],
         compiler_params=pltpu.CompilerParams(
             collective_id=0, has_side_effects=True, vmem_limit_bytes=62 * 2**20
         ),
         name="window",
-    )(query, key, value, grad, mask, text_key, text_value, text_mask)
+    )(query, key, value, grad, mask, text_query, text_key, text_value, text_grad, text_mask)
 
 
 def edge_mask(tile_lists, tile, slot):
@@ -565,116 +892,16 @@
     text_mask,
 ):
     frames, rows, width_tiles, tile, channels = query_latent.shape
-    head_dim = HD
-    heads = channels // head_dim
-    nh = heads // 2
-    score_scale = 1.0 / math.sqrt(head_dim)
-    text_on = text_mask > 0
-    key_text = text_key.reshape(-1, heads, head_dim)
-    value_text = text_value.reshape(-1, heads, head_dim)
-    query_text = text_query.reshape(-1, heads, head_dim)
-    grad_words = grad_text.reshape(-1, heads, head_dim)
-    t = lax.axis_index("tm")
-    h = lax.axis_index("height")
-    half = (t % 2 + h // (lax.axis_size("height") // 2)) % 2
     flat = [
         a.reshape(width_tiles * tile, channels)
         for a in (query_latent, key_latent, value_latent, grad_latent)
     ]
-    mask = edge_mask(tile_lists, tile, t % 2)
-    tm_cols = jnp.broadcast_to(text_on.astype(F32)[:, None], (text_on.shape[0], HD))
-    out_latent, grad_q_latent, win_dk, win_dv, td = window_pass(
-        *flat, mask, text_key, text_value, tm_cols
+    mask = edge_mask(tile_lists, tile, lax.axis_index("tm") % 2)
+    text_on = jnp.broadcast_to(
+        (text_mask > 0).astype(F32)[:, None], (text_mask.shape[0], HD)
     )
-    td = jnp.transpose(td, (1, 2, 0, 3)).reshape(2, -1, nh * head_dim)
-    wide = jnp.zeros((2, td.shape[1], channels), F32)
-    wide = lax.dynamic_update_slice(
-        wide, td, (jnp.int32(0), jnp.int32(0), (half * nh * head_dim).astype(jnp.int32))
-    )
-    text_dk, text_dv = wide[0], wide[1]
-
-    own_keys = key_latent.reshape(-1, heads, head_dim)
-    own_values = value_latent.reshape(-1, heads, head_dim)
-    score_own = (
-        jnp.einsum("ihd,jhd->hij", query_text, own_keys, preferred_element_type=F32) * score_scale
-    )
-    score_words = (
-        jnp.einsum("ihd,jhd->hij", query_text, key_text, preferred_element_type=F32) * score_scale
-    )
-    score_words = jnp.where(text_on[None, None, :], score_words, -jnp.inf)
-    local_peak = jnp.max(score_own, -1)
-    peak = lax.pmax(local_peak, ("tm", "height"))
-    peak = jnp.maximum(peak, jnp.max(score_words, -1))
-    local_total = jnp.sum(jnp.exp(score_own - peak[..., None]), -1)
-    total = lax.psum(local_total, ("tm", "height"))
-    total = total + jnp.sum(jnp.exp(score_words - peak[..., None]), -1)
-    log_total = (peak + jnp.log(total))[..., None]
-    prob_own = jnp.exp(score_own - log_total)
-    prob_words = jnp.exp(score_words - log_total)
-    weight_own = prob_own.astype(BF16)
-    weight_words = prob_words.astype(BF16)
-    numer = jnp.einsum(
-        "hij,jhd->ihd", weight_own, own_values, preferred_element_type=F32
-    ).reshape(-1, channels)
-    numer = lax.psum(numer, ("tm", "height"))
-    words_part = jnp.einsum(
-        "hij,jhd->ihd", weight_words, value_text, preferred_element_type=F32
-    ).reshape(-1, channels)
-    out_text = (numer + words_part).astype(BF16)
-    row_delta = jnp.transpose(
-        jnp.sum(grad_words.astype(F32) * out_text.reshape(-1, heads, head_dim).astype(F32), -1),
-        (1, 0),
-    )[..., None]
-    dscore_own = (
-        prob_own
-        * (
-            jnp.einsum("ihd,jhd->hij", grad_words, own_values, preferred_element_type=F32)
-            - row_delta
-        )
-    ).astype(BF16)
-    dscore_words = (
-        prob_words
-        * (
-            jnp.einsum("ihd,jhd->hij", grad_words, value_text, preferred_element_type=F32)
-            - row_delta
-        )
-    ).astype(BF16)
-    query_part = (
-        jnp.einsum("hij,jhd->ihd", dscore_own, own_keys, preferred_element_type=F32) * score_scale
-    )
-    own_dk = (
-        jnp.einsum("hij,ihd->jhd", dscore_own, query_text, preferred_element_type=F32)
-        * score_scale
-    )
-    own_dv = jnp.einsum("hij,ihd->jhd", weight_own, grad_words, preferred_element_type=F32)
-    summed_q, summed_k, summed_v = lax.psum(
-        (query_part.reshape(-1, channels), text_dk, text_dv), ("tm", "height")
-    )
-    words_q = (
-        jnp.einsum("hij,jhd->ihd", dscore_words, key_text, preferred_element_type=F32)
-        * score_scale
-    )
-    words_k = (
-        jnp.einsum("hij,ihd->jhd", dscore_words, query_text, preferred_element_type=F32)
-        * score_scale
-    )
-    words_v = jnp.einsum("hij,ihd->jhd", weight_words, grad_words, preferred_element_type=F32)
-    grad_q_text = (summed_q + words_q.reshape(-1, channels)).astype(BF16)
-    grad_k_text = (summed_k + words_k.reshape(-1, channels)).astype(BF16)
-    grad_v_text = (summed_v + words_v.reshape(-1, channels)).astype(BF16)
-    shape = query_latent.shape
-    grad_k_latent = (win_dk.astype(F32) + own_dk.reshape(win_dk.shape)).astype(BF16)
-    grad_v_latent = (win_dv.astype(F32) + own_dv.reshape(win_dv.shape)).astype(BF16)
-    return (
-        out_latent.reshape(shape),
-        grad_q_latent.reshape(shape),
-        grad_k_latent.reshape(shape),
-        grad_v_latent.reshape(shape),
-        out_text,
-        grad_q_text,
-        grad_k_text,
-        grad_v_text,
-    )
+    outs = window_pass(*flat, mask, text_query, text_key, text_value, grad_text, text_on)
+    return tuple(a.reshape(query_latent.shape) for a in outs[:4]) + tuple(outs[4:])
 
 
 def solution(mesh):

time: 684 us -> 271 us (0.40)
  blocking collectives: 356 us -> 0 us
  Pallas kernels: 138 us -> 252 us
  waiting for transfers between devices: 113 us -> 0 us
  matrix products: 18.2 us -> 0 us
  local copies, waits for them, and re-layouts: 29.6 us -> 12.1 us
  between operations: 14.5 us -> 0.73 us
  other arithmetic: 13.6 us -> 1.16 us
    pmax x1 -> x0, blocking collectives: 183 us -> none  [body(): peak = lax.pmax(local_peak, ('tm', 'height'))]
    psum x1 -> x0, blocking collectives: 174 us -> none  [body(): total = lax.psum(local_total, ('tm', 'height'))]
    pallas_call x1, Pallas kernels: 138 us -> 252 us  [window_pass(): pl.pallas_call(functools.partial(window_kernel, nx, ny), out_shape=[sds((...]
    psum x2 -> x0, waiting for transfers between devices: 113 us -> none  [the longest x1 113 us: body(): lax.psum((query_part.reshape(-1, channels), text_dk, text_dv), ('tm', 'he...]
    dot_general x12 -> x0, matrix products: 18.2 us -> none  [the longest x1 2.91 us: body(): jnp.einsum('hij,jhd->ihd', weight_own, own_values, preferred_element_type...]
    reshape x9 -> x0, local copies, waits for them, and re-layouts: 13 us -> none  [the longest x1 2.3 us: body(): grad_v_text = (summed_v + words_v.reshape(-1, channels)).astype(BF16)]
    convert_element_type x7 -> x1, other arithmetic: 11.1 us -> 0.01 us  [body(): (text_mask > 0).astype(F32)[:, None]]
  transfers between devices with their start and end apart: 2 -> 0, of which waited for: 1 -> 0; matrix products, arithmetic and copies ran while one was open for 5% -> 0% of each run, Pallas kernels for 20% -> 0%
where the time goes in v2:
time: 271 us; the launch traced here: 266 us
  Pallas kernels  252 us (93%)
  local copies, waits for them, and re-layouts  12.1 us (4%)
    pallas_call x1, Pallas kernels, window_pass(): pl.pallas_call(functools.partial(window_kernel, nx, ny), out_shape=[sds((...  252 us
    unnamed x28, local copies, waits for them, and re-layouts  11.1 us

profile of v2, /device:TPU:0, one launch (start us, length us, event | category | flops | bytes accessed | tf_op | source)
XLA Modules:
  0.0 266.4 jit_solution(1745630600391902167)
XLA Ops:
  0.7 0.7 copy-done.8
  1.3 0.0 copy-done.7
  1.3 0.1 reshape.54
  1.4 0.5 and_reduce_fusion.1
  2.0 0.1 copy.22
  2.1 0.1 broadcast_in_dim.4
  2.2 0.6 pad_select_fusion.mask_ref
  2.9 0.8 broadcast_in_dim.5.tm_ref
  3.6 252.4 %window.1 = (bf16[512,768]{1,0:T(8,128)(2,1)}, bf16[512,768]{1,0:T(8,128)(2,1)}, bf16[512,768]{1,0:T(8,128)(2,1)}, bf16[512,768]{1,0:T(8,128)(2,1)}, bf16[256,76...) custom-call(bf16[512,768]{1,0:T(8,128)(2,1)} %bitcast.17, ...), custom_call_target="tpu_custom_call" | custom-call | tf_op jit(solution)/shard_map/window/pallas_call | solution.py:805
  256.0 2.1 copy.34
  258.2 0.0 copy-done.2
  258.2 0.9 copy.35
  259.0 0.5 copy-done.1
  259.6 0.9 copy.36
  260.5 0.5 copy-done
  261.0 0.9 copy.37
  261.9 0.4 copy-done.6
  262.2 0.7 copy.38
  263.0 0.4 copy-done.5
  263.4 0.7 copy.39
  264.1 0.4 copy-done.4
  264.5 0.7 copy.40
  265.2 0.4 copy-done.3
  265.6 0.7 copy.41
  (15 shorter events, 0.1 us)
Async XLA Ops:
  0.6 0.7 copy-start.8
  0.7 0.7 copy-start.7
  256.0 2.1 copy-start.2
  258.2 1.4 copy-start.1
  259.6 1.4 copy-start
  261.0 1.2 copy-start.6
  262.2 1.1 copy-start.5
  263.4 1.1 copy-start.4
  264.5 1.1 copy-start.3

commit v3 on v1

--- a/solution.py
+++ b/solution.py
@@ -35,14 +35,19 @@
     v_ref,
     g_ref,
     mask_ref,
+    tq_ref,
     tk_ref,
     tv_ref,
+    tg_ref,
     tm_ref,
     out_ref,
     dq_ref,
     dk_ref,
     dv_ref,
-    td_ref,
+    tout_ref,
+    tdq_ref,
+    tdk_ref,
+    tdv_ref,
     kv,
     qg,
     mask,
@@ -59,6 +64,20 @@
     g1r,
     g2r,
     fin,
+    st,
+    lse,
+    part0,
+    gh0,
+    gx0,
+    whole0,
+    part,
+    gh,
+    gx,
+    gx2,
+    gh2,
+    whole,
+    t_kv,
+    t_fin,
     sem_loc,
     sem_r1s,
     sem_r1r,
@@ -74,6 +93,11 @@
     sem_g3s,
     sem_g3r,
     sem_out,
+    sem_txs,
+    sem_txr,
+    sem_tfs,
+    sem_tfr,
+    sem_tfl,
 ):
     bq = q_ref.shape[0]
     tile = bq // 4
@@ -93,43 +117,30 @@
     other = 1 - half
     rows_all = 2 * ny
 
-    def at_height(hh):
-        return (2 * x + (half + hh // ny) % 2, hh, c)
+    def at_grid(xx, hh):
+        return (2 * xx + (half + hh // ny) % 2, hh, c)
 
     partner = (2 * x + 1 - zl, h, c)
     left = (t - 2, h, c)
     right = (t + 2, h, c)
-    up = at_height(h - 1)
-    down = at_height(h + 1)
+    up = at_grid(x, h - 1)
+    down = at_grid(x, h + 1)
     has_left = x > 0
     has_right = x < nx - 1
     has_up = h > 0
     has_down = h < rows_all - 1
 
+    words_n = tq_ref.shape[0]
+    h_peers = [(j, (h + j + 1) % rows_all) for j in range(rows_all - 1)]
+    x_peers = [(j, (x + j + 1) % nx) for j in range(nx - 1)]
+
     barrier = pltpu.get_barrier_semaphore()
-    greet = [
-        (None, partner),
-        (has_left, left),
-        (has_right, right),
-        (has_up, up),
-        (has_down, down),
-    ]
-    for cond, dev in greet:
-        def hello(dev=dev):
-            pl.semaphore_signal(barrier, inc=1, device_id=dev, device_id_type=MESH)
-
-        if cond is None:
-            hello()
-        else:
-            pl.when(cond)(hello)
-    count = (
-        1
-        + has_left.astype(jnp.int32)
-        + has_right.astype(jnp.int32)
-        + has_up.astype(jnp.int32)
-        + has_down.astype(jnp.int32)
-    )
-    pl.semaphore_wait(barrier, count)
+    pl.semaphore_signal(barrier, inc=1, device_id=partner, device_id_type=MESH)
+    for _, to in h_peers:
+        pl.semaphore_signal(barrier, inc=1, device_id=at_grid(x, to), device_id_type=MESH)
+    for _, to in x_peers:
+        pl.semaphore_signal(barrier, inc=1, device_id=at_grid(to, h), device_id_type=MESH)
+    pl.semaphore_wait(barrier, nx + rows_all - 1)
 
     def remote(src, dst, ssem, rsem, dev):
         return pltpu.make_async_remote_copy(
@@ -165,10 +176,10 @@
     mask_out = remote(mask_ref, mask.at[:, mask_cols], sem_mask.at[0], sem_mask.at[1], partner)
     mask_own = pltpu.make_async_copy(mask_ref, mask.at[:, mask_cols], sem_mask.at[2])
 
-    def r2(i, d):
+    def r2(i, d, s):
         return remote(
-            kv.at[i, :, 1, pl.ds(1, 2)], kv.at[i, :, 2 - 2 * d, pl.ds(1, 2)],
-            sem_r2s.at[i, d], sem_r2r.at[i, d], (up, down)[d],
+            kv.at[i, :, 1, 1 + s], kv.at[i, :, 2 - 2 * d, 1 + s],
+            sem_r2s.at[i, d, s], sem_r2r.at[i, d, s], (up, down)[d],
         )
 
     def r3(i, r, d):
@@ -208,18 +219,36 @@
     side_on = (has_left, has_right)
     vert_on = (has_up, has_down)
 
-    def wait_r1(i):
-        for j in range(4):
+    def wait_in(i, which):
+        for j in which:
+            r1(i, j).wait_recv()
+
+    def wait_local(i, which):
+        for j in which:
             local_in(i, j).wait()
-            r1(i, j).wait_recv()
-
-    def start_r2(i):
+
+    def start_r2(i, s):
         for d in range(2):
-            pl.when(vert_on[d])(lambda d=d: r2(i, d).start())
+            pl.when(vert_on[d])(lambda d=d: r2(i, d, s).start())
 
     def wait_r2(i):
         for d in range(2):
-            pl.when(vert_on[1 - d])(lambda d=d: r2(i, d).wait_recv())
+            @pl.when(vert_on[1 - d])
+            def _(d=d):
+                r2(i, d, 0).wait_recv()
+                r2(i, d, 1).wait_recv()
+
+    def start_own(i):
+        wait_local(i, (1, 2))
+        start_r2(i, zl)
+        for d in range(2):
+            pl.when((zl == d) & side_on[d])(lambda d=d: r3(i, 1, d).start())
+
+    def start_traded(i):
+        wait_in(i, (1, 2))
+        start_r2(i, 1 - zl)
+        for d in range(2):
+            pl.when((zl != d) & side_on[d])(lambda d=d: r3(i, 1, d).start())
 
     def for_sides(i, rows, act, flip):
         for r in rows:
@@ -235,11 +264,242 @@
     def wait_r3(i):
         for_sides(i, (0, 1, 2), lambda i, r, d: r3(i, r, d).wait_recv(), True)
 
-    @pl.loop(0, nh)
-    def _(i):
-        for j in range(4):
+    first = (x == 0) & (h == 0)
+
+    per = words_n // rows_all // nx
+
+    class Round:
+        def __init__(self, n, src, got_outer, got_inner, dst, lo, hi, h_outer):
+            self.n, self.src, self.dst = n, src, dst
+            self.got_outer, self.got_inner = got_outer, got_inner
+            self.lo, self.hi, self.tiles = lo, hi, pl.ds(lo, hi - lo)
+            self.h_outer = h_outer
+            self.band = words_n // (rows_all if h_outer else nx)
+            self.me = (h, x) if h_outer else (x, h)
+            self.outer_peers = h_peers if h_outer else x_peers
+            self.inner_peers = x_peers if h_outer else h_peers
+
+        def device(self, o, i):
+            return at_grid(i, o) if self.h_outer else at_grid(o, i)
+
+        def rows(self, o):
+            return pl.ds(pl.multiple_of(o * self.band, 8), self.band)
+
+        def piece(self, o, i):
+            return pl.ds(pl.multiple_of(o * self.band + i * per, 8), per)
+
+        def own_rows(self):
+            return self.rows(self.me[0])
+
+        def own_piece(self):
+            return self.piece(*self.me)
+
+        def copies(self, stage):
+            o, i = self.me
+            if stage == 0:
+                pairs = [
+                    (self.src.at[self.tiles, self.rows(to)], self.got_outer.at[j], (to, i))
+                    for j, to in self.outer_peers
+                ]
+            elif stage == 1:
+                pairs = [
+                    (self.src.at[self.tiles, self.piece(o, to)], self.got_inner.at[j], (o, to))
+                    for j, to in self.inner_peers
+                ]
+            elif stage == 2:
+                own = self.dst.at[self.tiles, self.own_piece()]
+                pairs = [(own, own, (o, to)) for j, to in self.inner_peers]
+            else:
+                own = self.dst.at[self.tiles, self.own_rows()]
+                pairs = [(own, own, (to, i)) for j, to in self.outer_peers]
+            return [
+                remote(
+                    a, b, sem_txs.at[self.n, stage, j], sem_txr.at[self.n, stage, j],
+                    self.device(*to),
+                )
+                for j, (a, b, to) in enumerate(pairs)
+            ]
+
+        def send(self, stage):
+            for copy in self.copies(stage):
+                copy.start()
+
+        def got(self, stage):
+            for copy in self.copies(stage):
+                copy.wait_recv()
+
+        def sent(self):
+            for stage in range(4):
+                for copy in self.copies(stage):
+                    copy.wait_send()
+
+    round0 = Round(0, part0, gh0, gx0, whole0, 0, nh + 2, True)
+    round1 = Round(1, part, gh, gx, whole, 0, 3 * nh - 2, True)
+    round2 = Round(2, part, gx2, gh2, whole, 3 * nh - 2, 3 * nh, False)
+
+    def merged(own, parts):
+        peak = own(nh)
+        for p in parts:
+            peak = jnp.maximum(peak, p[nh])
+        f = jnp.exp2(own(nh) - peak)
+        total = own(nh + 1) * f
+        values = [own(i) * f[:, i : i + 1] for i in range(nh)]
+        for p in parts:
+            f = jnp.exp2(p[nh] - peak)
+            total = total + p[nh + 1] * f
+            values = [v + p[i] * f[:, i : i + 1] for i, v in enumerate(values)]
+        return values, peak, total
+
+    def merge0_outer():
+        round0.got(0)
+        at = round0.own_rows()
+        values, peak, total = merged(
+            lambda a: part0[a, at], [gh0.at[j] for j, _ in h_peers]
+        )
+        for i in range(nh):
+            part0[i, at] = values[i]
+        part0[nh, at] = peak
+        part0[nh + 1, at] = total
+        round0.send(1)
+
+    def merge0_inner():
+        round0.got(1)
+        at = round0.own_piece()
+        values, peak, total = merged(
+            lambda a: part0[a, at], [gx0.at[j] for j, _ in x_peers]
+        )
+        for i in range(nh):
+            value = values[i] / total[:, i : i + 1]
+            whole0[i, at] = value.astype(BF16).astype(F32)
+        whole0[nh, at] = peak + jnp.log2(total)
+        whole0[nh + 1, at] = total
+        round0.send(2)
+
+    def merge_outer(rnd):
+        rnd.got(0)
+        at = rnd.own_rows()
+        for a in range(rnd.lo, rnd.hi):
+            total = part[a, at]
+            for j, _ in rnd.outer_peers:
+                total = total + rnd.got_outer[j, a - rnd.lo]
+            part[a, at] = total
+        rnd.send(1)
+
+    def merge_inner(rnd):
+        rnd.got(1)
+        at = rnd.own_piece()
+        for a in range(rnd.lo, rnd.hi):
+            total = part[a, at]
+            for j, _ in rnd.inner_peers:
+                total = total + rnd.got_inner[j, a - rnd.lo]
+            whole[a, at] = total
+        rnd.send(2)
+
+    def spread(rnd):
+        rnd.got(2)
+        rnd.send(3)
+
+    def text_scores(i):
+        keys = kv[i, 0, 1, 1:3].reshape(both, HD)
+        return mm_nt(keys, tq_ref[:, head_cols(half, i)]) * c2
+
+    def words_scores(i):
+        cols = head_cols(half, i)
+        s = mm_nt(tk_ref[:, cols], tq_ref[:, cols]) * c2
+        return jnp.where(tm_ref[:, 0:1] > 0.5, s, NEG)
+
+    def text_partial(i):
+        def one(s, v, old):
+            peak = jnp.max(s, 0, keepdims=True)
+            if old is not None:
+                peak = jnp.maximum(peak, old[0])
+            e = jnp.exp2(s - peak)
+            total = jnp.sum(e, 0, keepdims=True)
+            value = mm_tn(v, e.astype(BF16))
+            if old is not None:
+                f = jnp.exp2(old[0] - peak)
+                total = total + old[1] * f
+                value = value + old[2].T * f
+            st[0, pl.ds(i, 1)] = peak
+            st[1, pl.ds(i, 1)] = total
+            part0[i] = value.T
+
+        one(text_scores(i), kv[i, 1, 1, 1:3].reshape(both, HD), None)
+
+        @pl.when(first)
+        def _():
+            old = (st[0, pl.ds(i, 1)], st[1, pl.ds(i, 1)], part0[i])
+            one(words_scores(i), tv_ref[:, head_cols(half, i)], old)
+
+    def text_start():
+        part0[nh] = st[0].T
+        part0[nh + 1] = st[1].T
+        round0.send(0)
+
+    def text_backward(i):
+        cols = head_cols(half, i)
+        row = lse[pl.ds(i, 1)]
+        q = tq_ref[:, cols]
+        g = tg_ref[:, cols]
+        o_round = whole0[i]
+        t_fin[0, i] = o_round.astype(BF16)
+        delta = jnp.sum((o_round * g.astype(F32)).T, 0, keepdims=True)
+
+        def one(s, k, v):
+            p = jnp.exp2(s - row)
+            ds = (p * (mm_nt(v, g) - delta)).astype(BF16)
+            return (
+                (mm_tn(k, ds) * scale).T,
+                mm_nn(ds, q) * scale,
+                mm_nn(p.astype(BF16), g),
+            )
+
+        a_q, a_k, a_v = one(
+            text_scores(i), kv[i, 0, 1, 1:3].reshape(both, HD), kv[i, 1, 1, 1:3].reshape(both, HD)
+        )
+        part[i] = a_q
+        t_kv[i, 0] = a_k
+        t_kv[i, 1] = a_v
+
+        @pl.when(first)
+        def _():
+            b_q, b_k, b_v = one(words_scores(i), tk_ref[:, cols], tv_ref[:, cols])
+            part[i] += b_q
+            part[nh + 2 * i] += b_k
+            part[nh + 2 * i + 1] += b_v
+
+    t_outs = (tout_ref, tdq_ref, tdk_ref, tdv_ref)
+
+    def t_out(j, i):
+        return remote(
+            t_fin.at[j, i], t_outs[j].at[:, head_cols(half, i)],
+            sem_tfs.at[j, i], sem_tfr.at[j, i], partner,
+        )
+
+    def t_loc(j, i):
+        return pltpu.make_async_copy(
+            t_fin.at[j, i], t_outs[j].at[:, head_cols(half, i)], sem_tfl.at[j, i]
+        )
+
+    def send_text(j, i):
+        t_out(j, i).start()
+        t_loc(j, i).start()
+
+    def finish_td(i):
+        for a in range(2):
+            t_fin[2 + a, i] = whole[nh + 2 * i + a].astype(BF16)
+            send_text(2 + a, i)
+
+    for i in range(nh):
+        for j in (1, 2):
+            local_in(i, j).start()
+    for i, js in ((0, (1, 2)), (0, (0, 3)), (1, (1, 2)), (2, (1, 2)), (1, (0, 3)), (2, (0, 3))):
+        for j in js:
             r1(i, j).start()
+    for i in range(nh):
+        for j in (0, 3):
             local_in(i, j).start()
+    start_own(0)
 
     mask_out.start()
     mask_own.start()
@@ -262,11 +522,15 @@
         def _():
             g2r[i, 1] = jnp.zeros(g2r.shape[2:], BF16)
 
+    @pl.loop(nh, 3 * nh)
+    def _(a):
+        part[a] = jnp.zeros(part.shape[1:], F32)
+
+    st[...] = jnp.zeros(st.shape, F32)
+    start_traded(0)
+    text_partial(0)
     mask_own.wait()
     mask_out.wait_recv()
-    wait_r1(0)
-    start_r2(0)
-    start_r3(0, (1,))
 
     def online(s, v, save, qs, keep):
         m_old = m_run[0:1, qs]
@@ -326,7 +590,7 @@
         share[i, 1, row, col] = d_v.astype(BF16)
 
     def add_g1(i):
-        for_sides(i, (0, 1, 2), lambda i, r, d: g1(i, r, d).wait_recv(), True)
+        for_sides(i, (0, 2), lambda i, r, d: g1(i, r, d).wait_recv(), True)
         for r in (0, 2):
             @pl.when(row_on(r))
             def _(r=r):
@@ -340,6 +604,7 @@
             pl.when(vert_on[d])(lambda d=d: g2(i, d).start())
 
     def add_g2(i):
+        for_sides(i, (1,), lambda i, r, d: g1(i, r, d).wait_recv(), True)
         for d in range(2):
             pl.when(vert_on[1 - d])(lambda d=d: g2(i, d).wait_recv())
         for a in range(2):
@@ -349,6 +614,7 @@
                     + g1r[i, 1 - s, a, 1].astype(F32)
                     + g2r[i, 0, a, s].astype(F32)
                     + g2r[i, 1, a, s].astype(F32)
+                    + t_kv[i, a, s * bq : (s + 1) * bq]
                 )
                 fin[i, 2 + a, s * bq : (s + 1) * bq] = total.astype(BF16)
         for j in (2, 3):
@@ -362,17 +628,24 @@
         o_t[...] = jnp.zeros(o_t.shape, F32)
         dq_t[...] = jnp.zeros(dq_t.shape, F32)
 
+        wait_local(i, (0, 3))
+        wait_in(i, (0, 3))
+
         @pl.loop(1, 3)
         def _(col):
             fwd_mid(i, 1, col)
 
         @pl.when(i == 0)
         def _():
-            wait_r1(1)
-            start_r2(1)
-            start_r3(1, (1,))
             wait_r2(0)
             start_r3(0, (0, 2))
+            start_own(1)
+            start_traded(1)
+            text_partial(1)
+
+        @pl.when(i == 1)
+        def _():
+            merge0_inner()
 
         @pl.loop(0, 4)
         def _(n):
@@ -384,14 +657,16 @@
 
         @pl.when(i == 0)
         def _():
-            wait_r1(2)
-            start_r2(2)
-            start_r3(2, (1,))
-
-        @pl.when(i < nh - 1)
-        def _():
-            wait_r2(i + 1)
-            start_r3(i + 1, (0, 2))
+            start_own(2)
+            start_traded(2)
+            text_partial(2)
+            text_start()
+            wait_r2(1)
+            start_r3(1, (0, 2))
+
+        @pl.when(i == 2)
+        def _():
+            merge_inner(round1)
 
         words = head_cols(half, i)
         s_text = jnp.where(
@@ -402,10 +677,6 @@
             p_text[...] = w
 
         online(s_text, tv_ref[:, words], 12, pl.ds(0, both), keep_text)
-
-        @pl.when(i > 0)
-        def _():
-            add_g1(i - 1)
 
         wait_r3(i)
         for d in range(2):
@@ -417,6 +688,20 @@
                     def _():
                         fwd_side(i, row, d)
 
+        @pl.when(i == 0)
+        def _():
+            wait_r2(2)
+            start_r3(2, (0, 2))
+            merge0_outer()
+
+        @pl.when(i == 1)
+        def _():
+            spread(round0)
+
+        @pl.when(i == 2)
+        def _():
+            spread(round1)
+
         inv = 1.0 / l_run[0:1, :]
         l_run[0:1, :] = inv
         o_round = (o_t[...] * inv).astype(BF16).astype(F32)
@@ -430,38 +715,90 @@
             p_text[...], tk_ref[:, words], tv_ref[:, words], qg[i, 0], qg[i, 1],
             12, pl.ds(0, both),
         )
-        td_ref[i, 0] = d_k
-        td_ref[i, 1] = d_v
+        part[nh + 2 * i] += d_k
+        part[nh + 2 * i + 1] += d_v
+
+        @pl.when(i == 2)
+        def _():
+            round2.send(0)
 
         for d in range(2):
             @pl.when(side_on[d])
             def _(d=d):
                 @pl.loop(0, 3)
-                def _(row):
+                def _(n):
+                    row = (2 * n) % 3
+
                     @pl.when(row_on(row))
                     def _():
                         bwd(i, row, 3 * d, pl.ds(d * bq, bq), p_side[row, d])
                         g1(i, row, d).start()
 
+            @pl.when(i == 2)
+            def _(d=d):
+                (merge_outer, merge_inner)[d](round2)
+
+        @pl.when(i == 1)
+        def _():
+            round0.got(3)
+            lse[...] = whole0[nh].T[0:8]
+
+            @pl.loop(0, nh)
+            def _(j):
+                text_backward(j)
+                send_text(0, j)
+
+            round1.send(0)
+
         @pl.when(i > 0)
         def _():
+            add_g1(i - 1)
+
+        @pl.when(i == 2)
+        def _():
+            spread(round2)
+
+        for stage, row in enumerate((0, 2, 1)):
+            @pl.when(row_on(row))
+            def _(row=row):
+                @pl.loop(1, 3)
+                def _(col):
+                    bwd(i, row, col, pl.ds(0, both), p_mid[row, col - 1])
+
+        @pl.when(i == 1)
+        def _():
+            merge_outer(round1)
+
+        @pl.when(i == 2)
+        def _():
+            round1.got(3)
+            for j in range(nh):
+                t_fin[1, j] = whole[j].astype(BF16)
+                send_text(1, j)
+            for j in range(nh - 1):
+                finish_td(j)
+
+        @pl.when(i > 0)
+        def _():
             add_g2(i - 1)
-
-        @pl.loop(0, 6)
-        def _(n):
-            row = n // 2
-            col = 1 + n % 2
-
-            @pl.when(row_on(row))
-            def _():
-                bwd(i, row, col, pl.ds(0, both), p_mid[row, col - 1])
 
         fin[i, 1] = (dq_t[...] * scale).T.astype(BF16)
         g3(i, 1).start()
         local_out(i, 1).start()
 
     add_g1(nh - 1)
+    round2.got(3)
+    finish_td(nh - 1)
     add_g2(nh - 1)
+
+    for rnd in (round0, round1, round2):
+        rnd.sent()
+
+    for n in range(4):
+        for j in range(nh):
+            t_out(n, j).wait_send()
+            t_out(n, j).wait_recv()
+            t_loc(n, j).wait()
 
     mask_out.wait_send()
 
@@ -475,13 +812,16 @@
         for d in range(2):
             @pl.when(vert_on[d])
             def _(d=d):
-                r2(i, d).wait_send()
+                r2(i, d, 0).wait_send()
+                r2(i, d, 1).wait_send()
                 g2(i, d).wait_send()
         for_sides(i, (0, 1, 2), lambda i, r, d: r3(i, r, d).wait_send(), False)
         for_sides(i, (0, 1, 2), lambda i, r, d: g1(i, r, d).wait_send(), False)
 
 
-def window_pass(query, key, value, grad, mask, text_key, text_value, text_mask):
+def window_pass(
+    query, key, value, grad, mask, text_query, text_key, text_value, text_grad, text_mask
+):
     nx = lax.axis_size("tm") // 2
     ny = lax.axis_size("height") // 2
     bq, channels = query.shape
@@ -494,9 +834,9 @@
     dma = pltpu.SemaphoreType.DMA
     return pl.pallas_call(
         functools.partial(window_kernel, nx, ny),
-        out_shape=[sds((bq, channels), BF16)] * 4 + [sds((nh, 2, words, HD), F32)],
-        in_specs=[hbm, hbm, hbm, hbm, vmem, vmem, vmem, vmem],
-        out_specs=[hbm] * 4 + [vmem],
+        out_shape=[sds((bq, channels), BF16)] * 4 + [sds((words, channels), BF16)] * 4,
+        in_specs=[hbm] * 4 + [vmem] * 6,
+        out_specs=[hbm] * 8,
         scratch_shapes=[
             pltpu.VMEM((nh, 2, 3, 4, bq, HD), BF16),
             pltpu.VMEM((nh, 2, both, HD), BF16),
@@ -514,12 +854,26 @@
             pltpu.VMEM((nh, 2, 2, 3, bq, HD), BF16),
             pltpu.VMEM((nh, 2, 2, 2, bq, HD), BF16),
             pltpu.VMEM((nh, 4, both, HD), BF16),
+            pltpu.VMEM((2, HD, words), F32),
+            pltpu.VMEM((8, words), F32),
+            pltpu.VMEM((nh + 2, words, HD), F32),
+            pltpu.VMEM((2 * ny - 1, nh + 2, words // (2 * ny), HD), F32),
+            pltpu.VMEM((nx - 1, nh + 2, words // (2 * ny * nx), HD), F32),
+            pltpu.VMEM((nh + 2, words, HD), F32),
+            pltpu.VMEM((3 * nh, words, HD), F32),
+            pltpu.VMEM((2 * ny - 1, 3 * nh - 2, words // (2 * ny), HD), F32),
+            pltpu.VMEM((nx - 1, 3 * nh - 2, words // (2 * ny * nx), HD), F32),
+            pltpu.VMEM((nx - 1, 2, words // nx, HD), F32),
+            pltpu.VMEM((2 * ny - 1, 2, words // (2 * ny * nx), HD), F32),
+            pltpu.VMEM((3 * nh, words, HD), F32),
+            pltpu.VMEM((nh, 2, both, HD), F32),
+            pltpu.VMEM((4, nh, words, HD), BF16),
             dma((nh, 4)),
             dma((nh, 4)),
             dma((nh, 4)),
             dma((3,)),
-            dma((nh, 2)),
-            dma((nh, 2)),
+            dma((nh, 2, 2)),
+            dma((nh, 2, 2)),
             dma((nh, 3, 2)),
             dma((nh, 3, 2)),
             dma((nh, 3, 2)),
@@ -529,12 +883,46 @@
             dma((nh, 4)),
             dma((nh, 4)),
             dma((nh, 4)),
+            dma((3, 4, 2 * ny - 1)),
+            dma((3, 4, 2 * ny - 1)),
+            dma((4, nh)),
+            dma((4, nh)),
+            dma((4, nh)),
         ],
         compiler_params=pltpu.CompilerParams(
             collective_id=0, has_side_effects=True, vmem_limit_bytes=62 * 2**20
         ),
         name="window",
-    )(query, key, value, grad, mask, text_key, text_value, text_mask)
+    )(query, key, value, grad, mask, text_query, text_key, text_value, text_grad, text_mask)
+
+
+def settle_kernel(*refs):
+    n = (len(refs) - 2) // 3
+    sems_in, sems_out = refs[-2:]
+    ins = [pltpu.make_async_copy(refs[j], refs[2 * n + j], sems_in.at[j]) for j in range(n)]
+    outs = [pltpu.make_async_copy(refs[2 * n + j], refs[n + j], sems_out.at[j]) for j in range(n)]
+    for copy in ins:
+        copy.start()
+    for j in range(n):
+        ins[j].wait()
+        outs[j].start()
+    for copy in outs:
+        copy.wait()
+
+
+def settle(arrays):
+    hbm = pl.BlockSpec(memory_space=pl.ANY)
+    n = len(arrays)
+    return pl.pallas_call(
+        settle_kernel,
+        out_shape=[jax.ShapeDtypeStruct(a.shape, a.dtype) for a in arrays],
+        in_specs=[hbm] * n,
+        out_specs=[hbm] * n,
+        scratch_shapes=[pltpu.VMEM(a.shape, a.dtype) for a in arrays]
+        + [pltpu.SemaphoreType.DMA((n,)), pltpu.SemaphoreType.DMA((n,))],
+        compiler_params=pltpu.CompilerParams(vmem_limit_bytes=62 * 2**20),
+        name="settle",
+    )(*arrays)
 
 
 def edge_mask(tile_lists, tile, slot):
@@ -565,116 +953,17 @@
     text_mask,
 ):
     frames, rows, width_tiles, tile, channels = query_latent.shape
-    head_dim = HD
-    heads = channels // head_dim
-    nh = heads // 2
-    score_scale = 1.0 / math.sqrt(head_dim)
-    text_on = text_mask > 0
-    key_text = text_key.reshape(-1, heads, head_dim)
-    value_text = text_value.reshape(-1, heads, head_dim)
-    query_text = text_query.reshape(-1, heads, head_dim)
-    grad_words = grad_text.reshape(-1, heads, head_dim)
-    t = lax.axis_index("tm")
-    h = lax.axis_index("height")
-    half = (t % 2 + h // (lax.axis_size("height") // 2)) % 2
     flat = [
         a.reshape(width_tiles * tile, channels)
         for a in (query_latent, key_latent, value_latent, grad_latent)
     ]
-    mask = edge_mask(tile_lists, tile, t % 2)
-    tm_cols = jnp.broadcast_to(text_on.astype(F32)[:, None], (text_on.shape[0], HD))
-    out_latent, grad_q_latent, win_dk, win_dv, td = window_pass(
-        *flat, mask, text_key, text_value, tm_cols
+    mask = edge_mask(tile_lists, tile, lax.axis_index("tm") % 2)
+    text_on = jnp.broadcast_to(
+        (text_mask > 0).astype(F32)[:, None], (text_mask.shape[0], HD)
     )
-    td = jnp.transpose(td, (1, 2, 0, 3)).reshape(2, -1, nh * head_dim)
-    wide = jnp.zeros((2, td.shape[1], channels), F32)
-    wide = lax.dynamic_update_slice(
-        wide, td, (jnp.int32(0), jnp.int32(0), (half * nh * head_dim).astype(jnp.int32))
-    )
-    text_dk, text_dv = wide[0], wide[1]
-
-    own_keys = key_latent.reshape(-1, heads, head_dim)
-    own_values = value_latent.reshape(-1, heads, head_dim)
-    score_own = (
-        jnp.einsum("ihd,jhd->hij", query_text, own_keys, preferred_element_type=F32) * score_scale
-    )
-    score_words = (
-        jnp.einsum("ihd,jhd->hij", query_text, key_text, preferred_element_type=F32) * score_scale
-    )
-    score_words = jnp.where(text_on[None, None, :], score_words, -jnp.inf)
-    local_peak = jnp.max(score_own, -1)
-    peak = lax.pmax(local_peak, ("tm", "height"))
-    peak = jnp.maximum(peak, jnp.max(score_words, -1))
-    local_total = jnp.sum(jnp.exp(score_own - peak[..., None]), -1)
-    total = lax.psum(local_total, ("tm", "height"))
-    total = total + jnp.sum(jnp.exp(score_words - peak[..., None]), -1)
-    log_total = (peak + jnp.log(total))[..., None]
-    prob_own = jnp.exp(score_own - log_total)
-    prob_words = jnp.exp(score_words - log_total)
-    weight_own = prob_own.astype(BF16)
-    weight_words = prob_words.astype(BF16)
-    numer = jnp.einsum(
-        "hij,jhd->ihd", weight_own, own_values, preferred_element_type=F32
-    ).reshape(-1, channels)
-    numer = lax.psum(numer, ("tm", "height"))
-    words_part = jnp.einsum(
-        "hij,jhd->ihd", weight_words, value_text, preferred_element_type=F32
-    ).reshape(-1, channels)
-    out_text = (numer + words_part).astype(BF16)
-    row_delta = jnp.transpose(
-        jnp.sum(grad_words.astype(F32) * out_text.reshape(-1, heads, head_dim).astype(F32), -1),
-        (1, 0),
-    )[..., None]
-    dscore_own = (
-        prob_own
-        * (
-            jnp.einsum("ihd,jhd->hij", grad_words, own_values, preferred_element_type=F32)
-            - row_delta
-        )
-    ).astype(BF16)
-    dscore_words = (
-        prob_words
-        * (
-            jnp.einsum("ihd,jhd->hij", grad_words, value_text, preferred_element_type=F32)
-            - row_delta
-        )
-    ).astype(BF16)
-    query_part = (
-        jnp.einsum("hij,jhd->ihd", dscore_own, own_keys, preferred_element_type=F32) * score_scale
-    )
-    own_dk = (
-        jnp.einsum("hij,ihd->jhd", dscore_own, query_text, preferred_element_type=F32)
-        * score_scale
-    )
-    own_dv = jnp.einsum("hij,ihd->jhd", weight_own, grad_words, preferred_element_type=F32)
-    summed_q, summed_k, summed_v = lax.psum(
-        (query_part.reshape(-1, channels), text_dk, text_dv), ("tm", "height")
-    )
-    words_q = (
-        jnp.einsum("hij,jhd->ihd", dscore_words, key_text, preferred_element_type=F32)
-        * score_scale
-    )
-    words_k = (
-        jnp.einsum("hij,ihd->jhd", dscore_words, query_text, preferred_element_type=F32)
-        * score_scale
-    )
-    words_v = jnp.einsum("hij,ihd->jhd", weight_words, grad_words, preferred_element_type=F32)
-    grad_q_text = (summed_q + words_q.reshape(-1, channels)).astype(BF16)
-    grad_k_text = (summed_k + words_k.reshape(-1, channels)).astype(BF16)
-    grad_v_text = (summed_v + words_v.reshape(-1, channels)).astype(BF16)
-    shape = query_latent.shape
-    grad_k_latent = (win_dk.astype(F32) + own_dk.reshape(win_dk.shape)).astype(BF16)
-    grad_v_latent = (win_dv.astype(F32) + own_dv.reshape(win_dv.shape)).astype(BF16)
-    return (
-        out_latent.reshape(shape),
-        grad_q_latent.reshape(shape),
-        grad_k_latent.reshape(shape),
-        grad_v_latent.reshape(shape),
-        out_text,
-        grad_q_text,
-        grad_k_text,
-        grad_v_text,
-    )
+    outs = window_pass(*flat, mask, text_query, text_key, text_value, grad_text, text_on)
+    outs = settle(outs)
+    return tuple(a.reshape(query_latent.shape) for a in outs[:4]) + tuple(outs[4:])
 
 
 def solution(mesh):

time: 684 us -> 217 us (0.32)
  blocking collectives: 356 us -> 0 us
  waiting for transfers between devices: 113 us -> 0 us
  Pallas kernels: 138 us -> 210 us
  local copies, waits for them, and re-layouts: 29.6 us -> 1.77 us
  matrix products: 18.2 us -> 0 us
  between operations: 14.5 us -> 0.87 us
  other arithmetic: 13.6 us -> 1.16 us
    pmax x1 -> x0, blocking collectives: 183 us -> none  [body(): peak = lax.pmax(local_peak, ('tm', 'height'))]
    psum x1 -> x0, blocking collectives: 174 us -> none  [body(): total = lax.psum(local_total, ('tm', 'height'))]
    psum x2 -> x0, waiting for transfers between devices: 113 us -> none  [the longest x1 113 us: body(): lax.psum((query_part.reshape(-1, channels), text_dk, text_dv), ('tm', 'he...]
    pallas_call x1, Pallas kernels: 138 us -> 206 us  [window_pass(): pl.pallas_call(functools.partial(window_kernel, nx, ny), out_shape=[sds((...]
    dot_general x12 -> x0, matrix products: 18.2 us -> none  [the longest x1 2.91 us: body(): jnp.einsum('hij,jhd->ihd', weight_own, own_values, preferred_element_type...]
    reshape x9 -> x0, local copies, waits for them, and re-layouts: 13 us -> none  [the longest x1 2.3 us: body(): grad_v_text = (summed_v + words_v.reshape(-1, channels)).astype(BF16)]
    unnamed x63 -> x6, local copies, waits for them, and re-layouts: 12.7 us -> 0.7 us
    convert_element_type x7 -> x1, other arithmetic: 11.1 us -> 0.01 us  [body(): (text_mask > 0).astype(F32)[:, None]]
  transfers between devices with their start and end apart: 2 -> 0, of which waited for: 1 -> 0; matrix products, arithmetic and copies ran while one was open for 5% -> 0% of each run, Pallas kernels for 20% -> 0%
where the time goes in v3:
time: 217 us; the launch traced here: 213 us
  Pallas kernels  210 us (97%)
    pallas_call x1, Pallas kernels, window_pass(): pl.pallas_call(functools.partial(window_kernel, nx, ny), out_shape=[sds((...  206 us

profile of v3, /device:TPU:0, one launch (start us, length us, event | category | flops | bytes accessed | tf_op | source)
XLA Modules:
  0.0 213.4 jit_solution(14621104251880212030)
XLA Ops:
  0.6 0.0 copy-start.1
  0.7 0.0 copy-start
  0.7 0.7 copy-done.1
  1.3 0.0 copy-done
  1.3 0.1 reshape.54
  1.4 0.5 and_reduce_fusion.1
  2.0 0.1 copy.22
  2.1 0.1 broadcast_in_dim.4
  2.2 0.6 pad_select_fusion.mask_ref
  2.9 0.8 broadcast_in_dim.5.tm_ref
  3.6 205.7 %window.1 = (bf16[512,768]{1,0:T(8,128)(2,1)}, bf16[512,768]{1,0:T(8,128)(2,1)}, bf16[512,768]{1,0:T(8,128)(2,1)}, bf16[512,768]{1,0:T(8,128)(2,1)}, bf16[256,76...) custom-call(bf16[512,768]{1,0:T(8,128)(2,1)} %bitcast.17, ...), custom_call_target="tpu_custom_call" | custom-call | tf_op jit(solution)/shard_map/window/pallas_call | solution.py:835
  209.4 3.8 %settle.1 = (bf16[512,768]{1,0:T(8,128)(2,1)}, bf16[512,768]{1,0:T(8,128)(2,1)}, bf16[512,768]{1,0:T(8,128)(2,1)}, bf16[512,768]{1,0:T(8,128)(2,1)}, bf16[256,76...) custom-call(bf16[512,768]{1,0:T(8,128)(2,1)} %get-tuple-element.24.refs_0_, ...), custom_call_target="tpu_custom_call" | custom-call | tf_op jit(solution)/shard_map/settle/pallas_call | solution.py:916
  (6 shorter events, 0.1 us)
Async XLA Ops:
  0.6 0.7 copy-start.1
  0.7 0.7 copy-start

commit v4 on v3

--- a/solution.py
+++ b/solution.py
@@ -71,10 +71,9 @@
     gx0,
     whole0,
     part,
+    part_b,
     gh,
     gx,
-    gx2,
-    gh2,
     whole,
     t_kv,
     t_fin,
@@ -266,58 +265,36 @@
 
     first = (x == 0) & (h == 0)
 
-    per = words_n // rows_all // nx
+    band = words_n // rows_all
+
+    def band_of(hh):
+        return pl.ds(pl.multiple_of(hh * band, 8), band)
+
+    own_band = band_of(h)
 
     class Round:
-        def __init__(self, n, src, got_outer, got_inner, dst, lo, hi, h_outer):
-            self.n, self.src, self.dst = n, src, dst
-            self.got_outer, self.got_inner = got_outer, got_inner
+        def __init__(self, n, first_src, src, got_h, got_x, dst, lo, hi):
+            self.n, self.first_src, self.src, self.dst = n, first_src, src, dst
+            self.got_h, self.got_x = got_h, got_x
             self.lo, self.hi, self.tiles = lo, hi, pl.ds(lo, hi - lo)
-            self.h_outer = h_outer
-            self.band = words_n // (rows_all if h_outer else nx)
-            self.me = (h, x) if h_outer else (x, h)
-            self.outer_peers = h_peers if h_outer else x_peers
-            self.inner_peers = x_peers if h_outer else h_peers
-
-        def device(self, o, i):
-            return at_grid(i, o) if self.h_outer else at_grid(o, i)
-
-        def rows(self, o):
-            return pl.ds(pl.multiple_of(o * self.band, 8), self.band)
-
-        def piece(self, o, i):
-            return pl.ds(pl.multiple_of(o * self.band + i * per, 8), per)
-
-        def own_rows(self):
-            return self.rows(self.me[0])
-
-        def own_piece(self):
-            return self.piece(*self.me)
 
         def copies(self, stage):
-            o, i = self.me
             if stage == 0:
-                pairs = [
-                    (self.src.at[self.tiles, self.rows(to)], self.got_outer.at[j], (to, i))
-                    for j, to in self.outer_peers
+                trips = [
+                    (self.first_src.at[self.tiles, band_of(to)], self.got_h.at[j, self.tiles], (x, to))
+                    for j, to in h_peers
                 ]
             elif stage == 1:
-                pairs = [
-                    (self.src.at[self.tiles, self.piece(o, to)], self.got_inner.at[j], (o, to))
-                    for j, to in self.inner_peers
-                ]
-            elif stage == 2:
-                own = self.dst.at[self.tiles, self.own_piece()]
-                pairs = [(own, own, (o, to)) for j, to in self.inner_peers]
+                own = self.src.at[self.tiles, own_band]
+                trips = [(own, self.got_x.at[j, self.tiles], (to, h)) for j, to in x_peers]
             else:
-                own = self.dst.at[self.tiles, self.own_rows()]
-                pairs = [(own, own, (to, i)) for j, to in self.outer_peers]
+                own = self.dst.at[self.tiles, own_band]
+                trips = [(own, own, (x, to)) for j, to in h_peers]
             return [
                 remote(
-                    a, b, sem_txs.at[self.n, stage, j], sem_txr.at[self.n, stage, j],
-                    self.device(*to),
+                    a, b, sem_txs.at[self.n, stage, j], sem_txr.at[self.n, stage, j], at_grid(*to)
                 )
-                for j, (a, b, to) in enumerate(pairs)
+                for j, (a, b, to) in enumerate(trips)
             ]
 
         def send(self, stage):
@@ -329,13 +306,13 @@
                 copy.wait_recv()
 
         def sent(self):
-            for stage in range(4):
+            for stage in range(3):
                 for copy in self.copies(stage):
                     copy.wait_send()
 
-    round0 = Round(0, part0, gh0, gx0, whole0, 0, nh + 2, True)
-    round1 = Round(1, part, gh, gx, whole, 0, 3 * nh - 2, True)
-    round2 = Round(2, part, gx2, gh2, whole, 3 * nh - 2, 3 * nh, False)
+    round0 = Round(0, part0, part0, gh0, gx0, whole0, 0, nh + 2)
+    round1 = Round(1, part_b, part, gh, gx, whole, 0, 3 * nh - 2)
+    round2 = Round(2, part_b, part, gh, gx, whole, 3 * nh - 2, 3 * nh)
 
     def merged(own, parts):
         peak = own(nh)
@@ -350,54 +327,51 @@
             values = [v + p[i] * f[:, i : i + 1] for i, v in enumerate(values)]
         return values, peak, total
 
-    def merge0_outer():
+    def merge0_h():
         round0.got(0)
-        at = round0.own_rows()
         values, peak, total = merged(
-            lambda a: part0[a, at], [gh0.at[j] for j, _ in h_peers]
+            lambda a: part0[a, own_band], [gh0.at[j] for j, _ in h_peers]
         )
         for i in range(nh):
-            part0[i, at] = values[i]
-        part0[nh, at] = peak
-        part0[nh + 1, at] = total
+            part0[i, own_band] = values[i]
+        part0[nh, own_band] = peak
+        part0[nh + 1, own_band] = total
         round0.send(1)
 
-    def merge0_inner():
+    def merge0_x():
         round0.got(1)
-        at = round0.own_piece()
         values, peak, total = merged(
-            lambda a: part0[a, at], [gx0.at[j] for j, _ in x_peers]
+            lambda a: part0[a, own_band], [gx0.at[j] for j, _ in x_peers]
         )
         for i in range(nh):
             value = values[i] / total[:, i : i + 1]
-            whole0[i, at] = value.astype(BF16).astype(F32)
-        whole0[nh, at] = peak + jnp.log2(total)
-        whole0[nh + 1, at] = total
+            whole0[i, own_band] = value.astype(BF16).astype(F32)
+        whole0[nh, own_band] = peak + jnp.log2(total)
+        whole0[nh + 1, own_band] = total
         round0.send(2)
 
-    def merge_outer(rnd):
+    def launch(rnd):
+        for a in range(rnd.lo, rnd.hi):
+            part_b[a] = part[a].astype(BF16)
+        rnd.send(0)
+
+    def merge_h(rnd):
         rnd.got(0)
-        at = rnd.own_rows()
         for a in range(rnd.lo, rnd.hi):
-            total = part[a, at]
-            for j, _ in rnd.outer_peers:
-                total = total + rnd.got_outer[j, a - rnd.lo]
-            part[a, at] = total
+            total = part[a, own_band]
+            for j, _ in h_peers:
+                total = total + gh[j, a].astype(F32)
+            part[a, own_band] = total
         rnd.send(1)
 
-    def merge_inner(rnd):
+    def merge_x(rnd):
         rnd.got(1)
-        at = rnd.own_piece()
         for a in range(rnd.lo, rnd.hi):
-            total = part[a, at]
-            for j, _ in rnd.inner_peers:
-                total = total + rnd.got_inner[j, a - rnd.lo]
-            whole[a, at] = total
+            total = part[a, own_band]
+            for j, _ in x_peers:
+                total = total + gx[j, a]
+            whole[a, own_band] = total.astype(BF16)
         rnd.send(2)
-
-    def spread(rnd):
-        rnd.got(2)
-        rnd.send(3)
 
     def text_scores(i):
         keys = kv[i, 0, 1, 1:3].reshape(both, HD)
@@ -487,7 +461,7 @@
 
     def finish_td(i):
         for a in range(2):
-            t_fin[2 + a, i] = whole[nh + 2 * i + a].astype(BF16)
+            t_fin[2 + a, i] = whole[nh + 2 * i + a]
             send_text(2 + a, i)
 
     for i in range(nh):
@@ -645,7 +619,7 @@
 
         @pl.when(i == 1)
         def _():
-            merge0_inner()
+            merge0_x()
 
         @pl.loop(0, 4)
         def _(n):
@@ -666,7 +640,7 @@
 
         @pl.when(i == 2)
         def _():
-            merge_inner(round1)
+            merge_x(round1)
 
         words = head_cols(half, i)
         s_text = jnp.where(
@@ -692,15 +666,7 @@
         def _():
             wait_r2(2)
             start_r3(2, (0, 2))
-            merge0_outer()
-
-        @pl.when(i == 1)
-        def _():
-            spread(round0)
-
-        @pl.when(i == 2)
-        def _():
-            spread(round1)
+            merge0_h()
 
         inv = 1.0 / l_run[0:1, :]
         l_run[0:1, :] = inv
@@ -720,7 +686,7 @@
 
         @pl.when(i == 2)
         def _():
-            round2.send(0)
+            launch(round2)
 
         for d in range(2):
             @pl.when(side_on[d])
@@ -732,15 +698,18 @@
                     @pl.when(row_on(row))
                     def _():
                         bwd(i, row, 3 * d, pl.ds(d * bq, bq), p_side[row, d])
-                        g1(i, row, d).start()
-
-            @pl.when(i == 2)
-            def _(d=d):
-                (merge_outer, merge_inner)[d](round2)
+
+            if d == 0:
+                @pl.when(i == 2)
+                def _():
+                    merge_h(round2)
+
+            for row in (0, 2, 1):
+                pl.when(side_on[d] & row_on(row))(lambda row=row, d=d: g1(i, row, d).start())
 
         @pl.when(i == 1)
         def _():
-            round0.got(3)
+            round0.got(2)
             lse[...] = whole0[nh].T[0:8]
 
             @pl.loop(0, nh)
@@ -748,32 +717,33 @@
                 text_backward(j)
                 send_text(0, j)
 
-            round1.send(0)
+            launch(round1)
 
         @pl.when(i > 0)
         def _():
             add_g1(i - 1)
 
-        @pl.when(i == 2)
-        def _():
-            spread(round2)
-
-        for stage, row in enumerate((0, 2, 1)):
+        for row in (0, 2, 1):
             @pl.when(row_on(row))
             def _(row=row):
                 @pl.loop(1, 3)
                 def _(col):
                     bwd(i, row, col, pl.ds(0, both), p_mid[row, col - 1])
 
+            if row == 2:
+                @pl.when(i == 2)
+                def _():
+                    merge_x(round2)
+
         @pl.when(i == 1)
         def _():
-            merge_outer(round1)
+            merge_h(round1)
 
         @pl.when(i == 2)
         def _():
-            round1.got(3)
+            round1.got(2)
             for j in range(nh):
-                t_fin[1, j] = whole[j].astype(BF16)
+                t_fin[1, j] = whole[j]
                 send_text(1, j)
             for j in range(nh - 1):
                 finish_td(j)
@@ -787,7 +757,7 @@
         local_out(i, 1).start()
 
     add_g1(nh - 1)
-    round2.got(3)
+    round2.got(2)
     finish_td(nh - 1)
     add_g2(nh - 1)
 
@@ -858,14 +828,13 @@
             pltpu.VMEM((8, words), F32),
             pltpu.VMEM((nh + 2, words, HD), F32),
             pltpu.VMEM((2 * ny - 1, nh + 2, words // (2 * ny), HD), F32),
-            pltpu.VMEM((nx - 1, nh + 2, words // (2 * ny * nx), HD), F32),
+            pltpu.VMEM((nx - 1, nh + 2, words // (2 * ny), HD), F32),
             pltpu.VMEM((nh + 2, words, HD), F32),
             pltpu.VMEM((3 * nh, words, HD), F32),
-            pltpu.VMEM((2 * ny - 1, 3 * nh - 2, words // (2 * ny), HD), F32),
-            pltpu.VMEM((nx - 1, 3 * nh - 2, words // (2 * ny * nx), HD), F32),
-            pltpu.VMEM((nx - 1, 2, words // nx, HD), F32),
-            pltpu.VMEM((2 * ny - 1, 2, words // (2 * ny * nx), HD), F32),
-            pltpu.VMEM((3 * nh, words, HD), F32),
+            pltpu.VMEM((3 * nh, words, HD), BF16),
+            pltpu.VMEM((2 * ny - 1, 3 * nh, words // (2 * ny), HD), BF16),
+            pltpu.VMEM((nx - 1, 3 * nh, words // (2 * ny), HD), F32),
+            pltpu.VMEM((3 * nh, words, HD), BF16),
             pltpu.VMEM((nh, 2, both, HD), F32),
             pltpu.VMEM((4, nh, words, HD), BF16),
             dma((nh, 4)),
@@ -883,8 +852,8 @@
             dma((nh, 4)),
             dma((nh, 4)),
             dma((nh, 4)),
-            dma((3, 4, 2 * ny - 1)),
-            dma((3, 4, 2 * ny - 1)),
+            dma((3, 3, 2 * ny - 1)),
+            dma((3, 3, 2 * ny - 1)),
             dma((4, nh)),
             dma((4, nh)),
             dma((4, nh)),

time: 217 us -> 194 us (0.89)
  Pallas kernels: 210 us -> 188 us
    pallas_call x1, Pallas kernels: 206 us -> 185 us  [window_pass(): pl.pallas_call(functools.partial(window_kernel, nx, ny), out_shape=[sds((...]
where the time goes in v4:
time: 194 us; the launch traced here: 192 us
  Pallas kernels  188 us (97%)
    pallas_call x1, Pallas kernels, window_pass(): pl.pallas_call(functools.partial(window_kernel, nx, ny), out_shape=[sds((...  185 us

profile of v4, /device:TPU:0, one launch (start us, length us, event | category | flops | bytes accessed | tf_op | source)
XLA Modules:
  0.0 192.2 jit_solution(15088409505716452774)
XLA Ops:
  0.6 0.0 copy-start.1
  0.7 0.0 copy-start
  0.7 0.7 copy-done.1
  1.3 0.0 copy-done
  1.3 0.1 reshape.54
  1.4 0.5 and_reduce_fusion.1
  2.0 0.1 copy.22
  2.1 0.1 broadcast_in_dim.4
  2.2 0.6 pad_select_fusion.mask_ref
  2.9 0.8 broadcast_in_dim.5.tm_ref
  3.6 184.5 %window.1 = (bf16[512,768]{1,0:T(8,128)(2,1)}, bf16[512,768]{1,0:T(8,128)(2,1)}, bf16[512,768]{1,0:T(8,128)(2,1)}, bf16[512,768]{1,0:T(8,128)(2,1)}, bf16[256,76...) custom-call(bf16[512,768]{1,0:T(8,128)(2,1)} %bitcast.17, ...), custom_call_target="tpu_custom_call" | custom-call | tf_op jit(solution)/shard_map/window/pallas_call | solution.py:805
  188.2 3.8 %settle.1 = (bf16[512,768]{1,0:T(8,128)(2,1)}, bf16[512,768]{1,0:T(8,128)(2,1)}, bf16[512,768]{1,0:T(8,128)(2,1)}, bf16[512,768]{1,0:T(8,128)(2,1)}, bf16[256,76...) custom-call(bf16[512,768]{1,0:T(8,128)(2,1)} %get-tuple-element.24.refs_0_, ...), custom_call_target="tpu_custom_call" | custom-call | tf_op jit(solution)/shard_map/settle/pallas_call | solution.py:885
  (6 shorter events, 0.1 us)
Async XLA Ops:
  0.6 0.7 copy-start.1
  0.7 0.7 copy-start

commit v5 on v4

--- a/solution.py
+++ b/solution.py
@@ -464,6 +464,8 @@
             t_fin[2 + a, i] = whole[nh + 2 * i + a]
             send_text(2 + a, i)
 
+    mask_out.start()
+    mask_own.start()
     for i in range(nh):
         for j in (1, 2):
             local_in(i, j).start()
@@ -475,8 +477,6 @@
             local_in(i, j).start()
     start_own(0)
 
-    mask_out.start()
-    mask_own.start()
 
     @pl.loop(0, nh)
     def _(i):

time: 194 us -> 169 us (0.87)
  Pallas kernels: 188 us -> 164 us
    pallas_call x1, Pallas kernels: 185 us -> 160 us  [window_pass(): pl.pallas_call(functools.partial(window_kernel, nx, ny), out_shape=[sds((...]
where the time goes in v5:
time: 169 us; the launch traced here: 167 us
  Pallas kernels  164 us (97%)
  local copies, waits for them, and re-layouts  1.77 us (1%)
    pallas_call x1, Pallas kernels, window_pass(): pl.pallas_call(functools.partial(window_kernel, nx, ny), out_shape=[sds((...  160 us
    pallas_call x1, Pallas kernels, settle(): pl.pallas_call(settle_kernel, out_shape=[jax.ShapeDtypeStruct(a.shape, a....  3.85 us

profile of v5, /device:TPU:0, one launch (start us, length us, event | category | flops | bytes accessed | tf_op | source)
XLA Modules:
  0.0 167.5 jit_solution(295431515160427312)
XLA Ops:
  0.6 0.0 copy-start.1
  0.7 0.0 copy-start
  0.7 0.7 copy-done.1
  1.3 0.0 copy-done
  1.3 0.1 reshape.54
  1.4 0.5 and_reduce_fusion.1
  2.0 0.1 copy.22
  2.1 0.1 broadcast_in_dim.4
  2.2 0.6 pad_select_fusion.mask_ref
  2.9 0.8 broadcast_in_dim.5.tm_ref
  3.6 159.8 %window.1 = (bf16[512,768]{1,0:T(8,128)(2,1)}, bf16[512,768]{1,0:T(8,128)(2,1)}, bf16[512,768]{1,0:T(8,128)(2,1)}, bf16[512,768]{1,0:T(8,128)(2,1)}, bf16[256,76...) custom-call(bf16[512,768]{1,0:T(8,128)(2,1)} %bitcast.17, ...), custom_call_target="tpu_custom_call" | custom-call | tf_op jit(solution)/shard_map/window/pallas_call | solution.py:805
  163.5 3.8 %settle.1 = (bf16[512,768]{1,0:T(8,128)(2,1)}, bf16[512,768]{1,0:T(8,128)(2,1)}, bf16[512,768]{1,0:T(8,128)(2,1)}, bf16[512,768]{1,0:T(8,128)(2,1)}, bf16[256,76...) custom-call(bf16[512,768]{1,0:T(8,128)(2,1)} %get-tuple-element.24.refs_0_, ...), custom_call_target="tpu_custom_call" | custom-call | tf_op jit(solution)/shard_map/settle/pallas_call | solution.py:885
  (6 shorter events, 0.1 us)
Async XLA Ops:
  0.6 0.7 copy-start.1
  0.7 0.7 copy-start

commit v6 on v5

--- a/solution.py
+++ b/solution.py
@@ -698,14 +698,16 @@
                     @pl.when(row_on(row))
                     def _():
                         bwd(i, row, 3 * d, pl.ds(d * bq, bq), p_side[row, d])
+                        if d == 1:
+                            g1(i, row, d).start()
 
             if d == 0:
                 @pl.when(i == 2)
                 def _():
                     merge_h(round2)
 
-            for row in (0, 2, 1):
-                pl.when(side_on[d] & row_on(row))(lambda row=row, d=d: g1(i, row, d).start())
+                for row in (0, 2, 1):
+                    pl.when(side_on[0] & row_on(row))(lambda row=row: g1(i, row, 0).start())
 
         @pl.when(i == 1)
         def _():

time: 169 us -> 169 us (level)
  no operation moved by 1% of the time
where the time goes in v6:
time: 169 us; the launch traced here: 167 us
  Pallas kernels  164 us (97%)
  local copies, waits for them, and re-layouts  1.77 us (1%)
    pallas_call x1, Pallas kernels, window_pass(): pl.pallas_call(functools.partial(window_kernel, nx, ny), out_shape=[sds((...  160 us
    pallas_call x1, Pallas kernels, settle(): pl.pallas_call(settle_kernel, out_shape=[jax.ShapeDtypeStruct(a.shape, a....  3.85 us

profile of v6, /device:TPU:0, one launch (start us, length us, event | category | flops | bytes accessed | tf_op | source)
XLA Modules:
  0.0 167.5 jit_solution(1360891572893704624)
XLA Ops:
  0.6 0.0 copy-start.1
  0.7 0.0 copy-start
  0.7 0.7 copy-done.1
  1.3 0.0 copy-done
  1.3 0.1 reshape.54
  1.4 0.5 and_reduce_fusion.1
  2.0 0.1 copy.22
  2.1 0.1 broadcast_in_dim.4
  2.2 0.6 pad_select_fusion.mask_ref
  2.9 0.8 broadcast_in_dim.5.tm_ref
  3.6 159.8 %window.1 = (bf16[512,768]{1,0:T(8,128)(2,1)}, bf16[512,768]{1,0:T(8,128)(2,1)}, bf16[512,768]{1,0:T(8,128)(2,1)}, bf16[512,768]{1,0:T(8,128)(2,1)}, bf16[256,76...) custom-call(bf16[512,768]{1,0:T(8,128)(2,1)} %bitcast.17, ...), custom_call_target="tpu_custom_call" | custom-call | tf_op jit(solution)/shard_map/window/pallas_call | solution.py:807
  163.5 3.8 %settle.1 = (bf16[512,768]{1,0:T(8,128)(2,1)}, bf16[512,768]{1,0:T(8,128)(2,1)}, bf16[512,768]{1,0:T(8,128)(2,1)}, bf16[512,768]{1,0:T(8,128)(2,1)}, bf16[256,76...) custom-call(bf16[512,768]{1,0:T(8,128)(2,1)} %get-tuple-element.24.refs_0_, ...), custom_call_target="tpu_custom_call" | custom-call | tf_op jit(solution)/shard_map/settle/pallas_call | solution.py:887
  (6 shorter events, 0.1 us)
Async XLA Ops:
  0.6 0.7 copy-start.1
  0.7 0.7 copy-start
